TPU v7x, 32 devices: a whole 2x2x4 slice. The times are simulated.
32 devices in a mesh: temporal: 4 (over z), spatial: 4 (over y, x), head: 2 (over core).
Axes of the slice: x: 2, y: 2, z: 4, core: 2. Of those that a mesh axis runs over, the one named last changes fastest.
Arguments:
- queries: bfloat16 [4096, 2048], P(('temporal', 'spatial'), 'head'), may hold values from -120 to 120
- keys: bfloat16 [4096, 2048], P(('temporal', 'spatial'), 'head'), may hold values from -6 to 6
- values: bfloat16 [4096, 2048], P(('temporal', 'spatial'), 'head'), may hold values from -6 to 6
- window: int32 [4, 1, 4, 27], P('temporal', None, 'spatial'), may hold values from 0 to 1, as said below
Outputs:
- attended: bfloat16 [4096, 2048], P(('temporal', 'spatial'), 'head')
Inputs may be any that keep to these rules, and one draw needn't show every extreme that they name: `window`: entry 9 (dt + 1) + 3 (dh + 1) + (dw + 1) of a tile's pattern admits the key tile at offset (dt, dh, dw) in tiles along frames, rows and columns; entry 13 is 1 for every tile.
All inputs are finite; a program needn't handle non-finite values.
Results may differ from a plain program's by a relative error of at most 0.0028.
Values may be sent and summed in bfloat16 or wider, within the bound.
A program may use at most 64 MiB of HBM per device.

v0:
```python
import math

import jax
import jax.numpy as jnp
from jax import lax
from jax.sharding import PartitionSpec as P

D_HEAD = 128
TILE_T = 4
TILE_H = 8
TILE_W = 8


def with_halo(array, sides, width):
    for axis, dim in sides:
        peers, length = (lax.axis_size(axis), array.shape[dim])
        up = [(i, (i + 1) % peers) for i in range(peers - 1)]
        down = [(j, i) for i, j in up]
        last = lax.slice_in_dim(array, length - width, length, axis=dim)
        initial = lax.slice_in_dim(array, 0, width, axis=dim)
        before = lax.ppermute(last, axis, up)
        after = lax.ppermute(initial, axis, down)
        array = jnp.concatenate([before, array, after], axis=dim)
    return array


def tile_mask(pattern, tile_row, first_row, window_rows, time_ok, width_ok):
    height_step = first_row - tile_row
    picked = [pattern[:, height_step + 1, :] == 1]
    chosen = jnp.stack(picked, axis=1)
    allowed = chosen & time_ok[:, None, None] & width_ok[None, None, :]
    return jnp.broadcast_to(
        allowed[:, None, :, None, :, None], (3, TILE_T, window_rows, TILE_H, 3, TILE_W)
    ).reshape(-1)


def attend(query_tile, key_window, value_window, key_ok):
    heads_here = query_tile.shape[1]
    group = min(2, heads_here)
    scale = 1.0 / math.sqrt(D_HEAD)
    pieces = []
    for head_start in range(0, heads_here, group):
        query_part = query_tile[:, head_start : head_start + group]
        key_part = key_window[:, head_start : head_start + group]
        value_part = value_window[:, head_start : head_start + group]
        scores = (
            jnp.einsum("qhd,khd->hqk", query_part, key_part, preferred_element_type=jnp.float32)
            * scale
        )
        scores = jnp.where(key_ok[None, None, :], scores, -jnp.inf)
        peak = jnp.max(scores, axis=-1, keepdims=True)
        weights = jnp.exp(scores - peak)
        total = jnp.sum(weights, axis=-1)
        attended_part = jnp.einsum(
            "hqk,khd->qhd",
            weights.astype(jnp.bfloat16),
            value_part,
            preferred_element_type=jnp.float32,
        )
        attended_part = attended_part / jnp.transpose(total)[:, :, None]
        pieces.append(attended_part.astype(jnp.bfloat16).reshape(attended_part.shape[0], -1))
    return jnp.concatenate(pieces, axis=1)


def body(queries, keys, values, window):
    space_count = lax.axis_size("spatial")
    time_count = lax.axis_size("temporal")
    tokens_dev, channels = queries.shape
    tile_rows = window.shape[1]
    height = tile_rows * TILE_H
    shard_rows = tokens_dev // (space_count * TILE_W)
    split = 1
    groups = space_count // split
    span = split * TILE_W
    part_channels = channels // split

    def to_blocks(tensor):
        shaped = tensor.reshape(shard_rows, groups, span, split, part_channels)
        return jnp.transpose(shaped, (3, 1, 0, 2, 4)).reshape(
            space_count, shard_rows, span, part_channels
        )

    def from_blocks(tensor):
        return tensor.reshape(TILE_T, height, span, part_channels)

    query_block, key_block, value_block = (
        lax.all_to_all(to_blocks(queries), "spatial", split_axis=0, concat_axis=0, tiled=True),
        lax.all_to_all(to_blocks(keys), "spatial", split_axis=0, concat_axis=0, tiled=True),
        lax.all_to_all(to_blocks(values), "spatial", split_axis=0, concat_axis=0, tiled=True),
    )
    add_key_block = from_blocks(key_block)
    add_value_block = from_blocks(value_block)
    paired = jnp.stack([add_key_block, add_value_block]).reshape(
        2, 1, TILE_T, height, split, TILE_W, part_channels
    )
    padded = with_halo(paired, (("temporal", 1), ("spatial", 4)), 1)
    query_block = from_blocks(query_block)
    column_base = lax.axis_index("spatial")
    offsets = jnp.arange(3, dtype=jnp.int32) - 1
    time_index = lax.axis_index("temporal") + offsets
    time_ok = (time_index >= 0) & (time_index < time_count)
    window_rows = min(3, tile_rows)
    heads_here = part_channels // D_HEAD
    width_index = column_base + 0 + offsets
    width_ok = (width_index >= 0) & (width_index < space_count)
    pattern_column = lax.dynamic_index_in_dim(window, 0, 2, keepdims=False)
    pattern_rows = pattern_column.reshape(tile_rows, 3, 3, 3)
    first_row = min(max(0 - 1, 0), tile_rows - window_rows)
    key_ok = tile_mask(pattern_rows[0], 0, first_row, window_rows, time_ok, width_ok)
    query_tile = query_block.reshape(-1, heads_here, D_HEAD)
    row_low = first_row * TILE_H
    row_high = row_low + window_rows * TILE_H
    key_window = padded[0, :, :, row_low:row_high, 0:3].reshape(-1, heads_here, D_HEAD)
    value_window = padded[1, :, :, row_low:row_high, 0:3].reshape(-1, heads_here, D_HEAD)
    attended_tile = attend(query_tile, key_window, value_window, key_ok)
    outputs = attended_tile.reshape(TILE_T, TILE_H, TILE_W, part_channels)
    result = outputs.reshape(space_count, shard_rows, span, part_channels)
    returned = lax.all_to_all(result, "spatial", split_axis=0, concat_axis=0, tiled=True)
    shaped = returned.reshape(split, groups, shard_rows, span, part_channels)
    return jnp.transpose(shaped, (2, 1, 3, 0, 4)).reshape(tokens_dev, channels)


def solution(mesh):
    return jax.shard_map(
        body,
        mesh=mesh,
        in_specs=(
            P(("temporal", "spatial"), "head"),
            P(("temporal", "spatial"), "head"),
            P(("temporal", "spatial"), "head"),
            P("temporal", None, "spatial", None),
        ),
        out_specs=P(("temporal", "spatial"), "head"),
        check_vma=False,
    )
```

profile of v0, /device:TPU:0, one launch (start us, length us, event | category | flops | bytes accessed | tf_op | source)
XLA Modules:
  0.0 258.4 jit_solution(16714366001775694003)
XLA Ops:
  0.0 1.9 copy.60
  1.9 5.2 %all-to-all-start = ((bf16[4,8,8,1024]{3,2,1,0:T(8,128)(2,1)}), bf16[4,8,8,1024]{3,2,1,0:T(8,128)(2,1)S(1)}, u32[]{:S(2)}, u32[]{:S(2)}) async-start(bf16[4,8,8,1024]{3,2,1,0:T(8,128)(2,1)} %copy.60), calls=%async_computation | async-start | bytes 1048576 | tf_op jit(solution)/shard_map/all_to_all | solution.py:88
  7.0 1.1 copy.61
  8.1 6.9 %all-to-all-done = bf16[4,8,8,1024]{3,2,1,0:T(8,128)(2,1)S(1)} async-done(((bf16[4,8,8,1024]{3,2,1,0:T(8,128)(2,1)}), bf16[4,8,8,1024]{3,2,1,0:T(8,128)(2,1)S(1)}, u32[]{:S(2)}, u32[]{:S(2)}) %all-to-all-start) | async-done | bytes 524320 | tf_op jit(solution)/shard_map/all_to_all | solution.py:88
  15.1 10.2 %all_to_all.20 = bf16[4,8,8,1024]{3,2,1,0:T(8,128)(2,1)S(1)} all-to-all(bf16[4,8,8,1024]{3,2,1,0:T(8,128)(2,1)S(1)} %copy.61), channel_id=1, replica_groups=mesh['temporal'=4,'spatial'=4,'head'=2] {'spatial'}, dimensions={0} | all-to-all | bytes 1048576 | tf_op jit(solution)/shard_map/all_to_all | solution.py:89
  25.4 3.7 %collective-permute-start = (bf16[2,1,4,8,1,8,1024]{6,5,3,2,0,4,1:T(8,128)(2,1)S(1)}, bf16[2,1,4,8,1,8,1024]{6,5,3,2,0,4,1:T(8,128)(2,1)S(1)}, u32[]{:S(2)}, u32[]{:S(2)}) collective-permute-start(bf16[2,1,4,8,1,8,1024]{6,5,3,2,0,4,1:T(8,128)(2,1)S(1)} %maximum_bitcast_fusion), channel_id=1, source_target_pairs={{0,8},{8,16},{16,24},{1,9},{9,17},{17,25},{2,10},{10,18},{18,26},{... | collective-permute-start | bytes 3145736 | tf_op jit(solution)/shard_map/ppermute | solution.py:21
  29.1 1.3 collective-permute-start.1
  30.4 18.3 %collective-permute-done = bf16[2,1,4,8,1,8,1024]{6,5,3,2,0,4,1:T(8,128)(2,1)S(1)} collective-permute-done((bf16[2,1,4,8,1,8,1024]{6,5,3,2,0,4,1:T(8,128)(2,1)S(1)}, bf16[2,1,4,8,1,8,1024]{6,5,3,2,0,4,1:T(8,128)(2,1)S(1)}, u32[]{:S(2)}, u32[]{:S(2)}) %collective-permute-start) | collective-permute-done | bytes 1048608 | tf_op jit(solution)/shard_map/ppermute | solution.py:21
  48.6 4.2 %collective-permute-done.1 = bf16[2,1,4,8,1,8,1024]{6,5,3,2,0,4,1:T(8,128)(2,1)S(1)} collective-permute-done((bf16[2,1,4,8,1,8,1024]{6,5,3,2,0,4,1:T(8,128)(2,1)S(1)}, bf16[2,1,4,8,1,8,1024]{6,5,3,2,0,4,1:T(8,128)(2,1)S(1)}, u32[]{:S(2)}, u32[]{:S(2)}) %collective-permute-start.1) | collective-permute-done | bytes 1048608 | tf_op jit(solution)/shard_map/ppermute | solution.py:22
  52.8 2.0 pad_maximum_fusion.1
  54.8 3.3 %collective-permute-start.2 = (bf16[2,3,4,8,1,8,1024]{6,5,3,2,0,4,1:T(8,128)(2,1)}, bf16[2,3,4,8,1,8,1024]{6,5,3,2,0,4,1:T(8,128)(2,1)S(1)}, u32[]{:S(2)}, u32[]{:S(2)}) collective-permute-start(bf16[2,3,4,8,1,8,1024]{6,5,3,2,0,4,1:T(8,128)(2,1)} %pad_maximum_fusion.1), channel_id=1, source_target_pairs={{0,2},{2,4},{4,6},{1,3},{3,5},{5,7},{8,10},{10,12},{12,14},{9,11},... | collective-permute-start | bytes 9437192 | tf_op jit(solution)/shard_map/ppermute | solution.py:21
  58.1 1.3 collective-permute-start.3
  59.4 0.8 copy.172
  60.3 5.7 %all-to-all-start.2 = ((bf16[4,8,8,1024]{3,2,1,0:T(8,128)(2,1)}), bf16[4,8,8,1024]{3,2,1,0:T(8,128)(2,1)}, u32[]{:S(2)}, u32[]{:S(2)}) async-start(bf16[4,8,8,1024]{3,2,1,0:T(8,128)(2,1)} %bitcast.83), calls=%async_computation.2 | async-start | bytes 1048576 | tf_op jit(solution)/shard_map/all_to_all | solution.py:87
  65.9 0.5 broadcast.96
  66.5 0.6 reduce.3
  67.4 0.1 broadcast_in_dim.46
  67.5 129.9 %all-to-all-done.2 = bf16[4,8,8,1024]{3,2,1,0:T(8,128)(2,1)} async-done(((bf16[4,8,8,1024]{3,2,1,0:T(8,128)(2,1)}), bf16[4,8,8,1024]{3,2,1,0:T(8,128)(2,1)}, u32[]{:S(2)}, u32[]{:S(2)}) %all-to-all-start.2) | async-done | bytes 524320 | tf_op jit(solution)/shard_map/all_to_all | solution.py:87
  197.4 1.1 copy.105
  198.6 1.1 fusion.103
  199.7 1.7 copy-done.3
  201.4 4.7 %pad_maximum_fusion = bf16[2,3,4,8,3,8,1024]{6,5,3,2,0,4,1:T(8,128)(2,1)S(1)} fusion(bf16[2,3,4,8,1,8,1024]{6,5,3,2,0,4,1:T(8,128)(2,1)} %collective-permute-done.3, bf16[2,1,4,8,1,8,1024]{6,5,3,2,0,4,1:T(8,128)(2,1)} %copy-done.2, bf16[2,1,4,8,1,8,1024]{6,5,3,2,0,4,1:T(8,128)(2,1)} %copy-done, bf16[2,1,4,8,1,8,1024]{6,5,3,2,0,4,1:T(8,128)(2,1)} %copy-done.1, ...), kind=kLoop, calls=%fused_computation | loop fusion | flops 18874368 | bytes 18874368 | tf_op jit(solution)/shard_map/concatenate | solution.py:23
  206.1 4.7 %fusion.100 = (bf16[1,3,4,8,3,8,1024]{6,5,3,2,0,4,1:T(8,128)(2,1)}, bf16[1,3,4,8,3,8,1024]{6,5,3,2,0,4,1:T(8,128)(2,1)}) fusion(bf16[2,3,4,8,3,8,1024]{6,5,3,2,0,4,1:T(8,128)(2,1)S(1)} %pad_maximum_fusion), kind=kLoop, calls=%fused_computation.66 | loop fusion | bytes 18874368 | tf_op jit(solution)/shard_map/slice | solution.py:114
  210.8 2.8 %copy.64 = bf16[1,3,4,8,3,8,1024]{6,5,4,3,2,1,0:T(8,128)(2,1)S(1)} copy(bf16[1,3,4,8,3,8,1024]{6,5,3,2,0,4,1:T(8,128)(2,1)} %get-tuple-element.6) | data formatting | bytes 9437184 | tf_op jit(solution)/shard_map/slice | solution.py:113
  213.7 1.3 copy.104
  215.0 4.6 %fusion.102 = (bf16[2304,2,128]{2,1,0:T(2,128)(2,1)S(1)}, bf16[2304,2,128]{2,1,0:T(2,128)(2,1)}, bf16[2304,2,128]{2,1,0:T(2,128)(2,1)}, bf16[2304,2,128]{2,1,0:T(2,128)(2,1)}) fusion(bf16[2304,8,128]{2,1,0:T(8,128)(2,1)S(1)} %bitcast.77), kind=kLoop, calls=%fused_computation.68 | loop fusion | bytes 9437184 | tf_op jit(solution)/shard_map/slice | solution.py:44
  219.6 0.7 copy.62
  220.3 1.2 copy.103
  221.6 3.4 %fusion.101 = (bf16[2304,2,128]{2,1,0:T(2,128)(2,1)S(1)}, bf16[2304,2,128]{2,1,0:T(2,128)(2,1)S(1)}, bf16[2304,2,128]{2,1,0:T(2,128)(2,1)S(1)}, bf16[2304,2,128]{2,1,0:T(2,128)(2,1)S(1)}) fusion(bf16[2304,8,128]{2,1,0:T(8,128)(2,1)S(1)} %bitcast.78), kind=kLoop, calls=%fused_computation.67 | loop fusion | bytes 9437184 | tf_op jit(solution)/shard_map/slice | solution.py:45
  225.0 0.8 fusion.107
  225.8 0.6 fusion.8
  226.4 1.6 fusion.91
  228.0 1.7 copy.69
  229.7 1.7 concatenate.20
  231.4 2.9 %fusion.106 = (f32[2,256]{1,0:T(2,128)S(1)}, f32[2,256,2304]{1,2,0:T(8,128)S(1)}) fusion(bf16[256,2,128]{2,1,0:T(2,128)(2,1)} %get-tuple-element.17, bf16[2304,2,128]{2,1,0:T(2,128)(2,1)} %get-tuple-element.13, pred[2304]{0:T(1024)(128)(4,1)S(1)} %broadcast_in_dim.46), kind=kOutput, calls=%fused_computation.72 | convolution fusion | flops 305528320 | bytes 6033664 | tf_op jit(solution)/shard_map/qhd,khd->hqk/dot_general | solution.py:47
  234.3 0.6 fusion.10
  234.9 1.6 fusion.81
  236.5 1.0 copy.74
  237.5 0.7 concatenate.21
  238.3 2.7 %fusion.105 = (f32[2,256]{1,0:T(2,128)S(1)}, f32[2,256,2304]{1,2,0:T(8,128)S(1)}) fusion(bf16[256,2,128]{2,1,0:T(2,128)(2,1)} %get-tuple-element.16, bf16[2304,2,128]{2,1,0:T(2,128)(2,1)} %get-tuple-element.12, pred[2304]{0:T(1024)(128)(4,1)S(1)} %broadcast_in_dim.46), kind=kOutput, calls=%fused_computation.71 | convolution fusion | flops 305528320 | bytes 6033664 | tf_op jit(solution)/shard_map/qhd,khd->hqk/dot_general | solution.py:47
  241.0 0.6 fusion.12
  241.7 1.6 fusion.71
  243.3 1.0 copy.79
  244.4 1.7 fusion.104
  246.1 0.6 fusion.14
  246.8 0.9 fusion.61
  248.0 9.5 %all_to_all.21 = bf16[4,8,8,1024]{3,2,1,0:T(8,128)(2,1)S(1)} all-to-all(bf16[4,8,8,1024]{3,2,1,0:T(8,128)(2,1)S(1)} %pad_maximum_fusion.2), channel_id=1, replica_groups=mesh['temporal'=4,'spatial'=4,'head'=2] {'spatial'}, dimensions={0} | all-to-all | bytes 1048576 | tf_op jit(solution)/shard_map/all_to_all | solution.py:118
  257.5 0.8 copy.85
  (36 shorter events, 0.8 us)
Async XLA Ops:
  1.9 13.2 %all-to-all-start = ((bf16[4,8,8,1024]{3,2,1,0:T(8,128)(2,1)}), bf16[4,8,8,1024]{3,2,1,0:T(8,128)(2,1)S(1)}, u32[]{:S(2)}, u32[]{:S(2)}) async-start(bf16[4,8,8,1024]{3,2,1,0:T(8,128)(2,1)} %copy.60), calls=%async_computation | async-start | bytes 1048576 | tf_op jit(solution)/shard_map/all_to_all | solution.py:88
  15.1 44.4 %copy-start.5 = (bf16[256,1024]{1,0:T(8,128)(2,1)S(1)}, bf16[256,1024]{1,0:T(8,128)(2,1)}, u32[]{:S(2)}) copy-start(bf16[256,1024]{1,0:T(8,128)(2,1)} %param.4) | copy-start | bytes 1572868
  25.3 27.5 %copy-start = (bf16[2,1,4,8,1,8,1024]{6,5,3,2,0,4,1:T(8,128)(2,1)}, bf16[2,1,4,8,1,8,1024]{6,5,3,2,0,4,1:T(8,128)(2,1)S(1)}, u32[]{:S(2)}) copy-start(bf16[2,1,4,8,1,8,1024]{6,5,3,2,0,4,1:T(8,128)(2,1)S(1)} %maximum_bitcast_fusion) | copy-start | bytes 3145732
  25.3 41.1 %copy-start.9 = (s32[1,1,1,27]{3,2,1,0:T(1,128)S(1)}, s32[1,1,1,27]{3,2,1,0:T(1,128)}, u32[]{:S(2)}) copy-start(s32[1,1,1,27]{3,2,1,0:T(1,128)} %param.7) | copy-start | bytes 328
  25.4 23.3 %collective-permute-start = (bf16[2,1,4,8,1,8,1024]{6,5,3,2,0,4,1:T(8,128)(2,1)S(1)}, bf16[2,1,4,8,1,8,1024]{6,5,3,2,0,4,1:T(8,128)(2,1)S(1)}, u32[]{:S(2)}, u32[]{:S(2)}) collective-permute-start(bf16[2,1,4,8,1,8,1024]{6,5,3,2,0,4,1:T(8,128)(2,1)S(1)} %maximum_bitcast_fusion), channel_id=1, source_target_pairs={{0,8},{8,16},{16,24},{1,9},{9,17},{17,25},{2,10},{10,18},{18,26},{... | collective-permute-start | bytes 3145736 | tf_op jit(solution)/shard_map/ppermute | solution.py:21
  29.1 23.8 %collective-permute-start.1 = (bf16[2,1,4,8,1,8,1024]{6,5,3,2,0,4,1:T(8,128)(2,1)S(1)}, bf16[2,1,4,8,1,8,1024]{6,5,3,2,0,4,1:T(8,128)(2,1)S(1)}, u32[]{:S(2)}, u32[]{:S(2)}) collective-permute-start(bf16[2,1,4,8,1,8,1024]{6,5,3,2,0,4,1:T(8,128)(2,1)S(1)} %maximum_bitcast_fusion), channel_id=1, source_target_pairs={{8,0},{16,8},{24,16},{9,1},{17,9},{25,17},{10,2},{18,10},{26,18},{... | collective-permute-start | bytes 3145736 | tf_op jit(solution)/shard_map/ppermute | solution.py:22
  48.6 6.2 %copy-start.1 = (bf16[2,1,4,8,1,8,1024]{6,5,3,2,0,4,1:T(8,128)(2,1)}, bf16[2,1,4,8,1,8,1024]{6,5,3,2,0,4,1:T(8,128)(2,1)S(1)}, u32[]{:S(2)}) copy-start(bf16[2,1,4,8,1,8,1024]{6,5,3,2,0,4,1:T(8,128)(2,1)S(1)} %collective-permute-done) | copy-start | bytes 3145732
  52.8 5.3 %copy-start.2 = (bf16[2,1,4,8,1,8,1024]{6,5,3,2,0,4,1:T(8,128)(2,1)}, bf16[2,1,4,8,1,8,1024]{6,5,3,2,0,4,1:T(8,128)(2,1)S(1)}, u32[]{:S(2)}) copy-start(bf16[2,1,4,8,1,8,1024]{6,5,3,2,0,4,1:T(8,128)(2,1)S(1)} %collective-permute-done.1) | copy-start | bytes 3145732
  54.8 144.9 %collective-permute-start.2 = (bf16[2,3,4,8,1,8,1024]{6,5,3,2,0,4,1:T(8,128)(2,1)}, bf16[2,3,4,8,1,8,1024]{6,5,3,2,0,4,1:T(8,128)(2,1)S(1)}, u32[]{:S(2)}, u32[]{:S(2)}) collective-permute-start(bf16[2,3,4,8,1,8,1024]{6,5,3,2,0,4,1:T(8,128)(2,1)} %pad_maximum_fusion.1), channel_id=1, source_target_pairs={{0,2},{2,4},{4,6},{1,3},{3,5},{5,7},{8,10},{10,12},{12,14},{9,11},... | collective-permute-start | bytes 9437192 | tf_op jit(solution)/shard_map/ppermute | solution.py:21
  58.1 143.3 %collective-permute-start.3 = (bf16[2,3,4,8,1,8,1024]{6,5,3,2,0,4,1:T(8,128)(2,1)}, bf16[2,3,4,8,1,8,1024]{6,5,3,2,0,4,1:T(8,128)(2,1)}, u32[]{:S(2)}, u32[]{:S(2)}) collective-permute-start(bf16[2,3,4,8,1,8,1024]{6,5,3,2,0,4,1:T(8,128)(2,1)} %pad_maximum_fusion.1), channel_id=1, source_target_pairs={{2,0},{4,2},{6,4},{3,1},{5,3},{7,5},{10,8},{12,10},{14,12},{11,9},... | collective-permute-start | bytes 9437192 | tf_op jit(solution)/shard_map/ppermute | solution.py:22
  60.3 137.2 %all-to-all-start.2 = ((bf16[4,8,8,1024]{3,2,1,0:T(8,128)(2,1)}), bf16[4,8,8,1024]{3,2,1,0:T(8,128)(2,1)}, u32[]{:S(2)}, u32[]{:S(2)}) async-start(bf16[4,8,8,1024]{3,2,1,0:T(8,128)(2,1)} %bitcast.83), calls=%async_computation.2 | async-start | bytes 1048576 | tf_op jit(solution)/shard_map/all_to_all | solution.py:87
  199.7 1.7 copy-start.3
  213.7 5.9 %slice-start = ((s8[4718592]{0:T(1024)(128)(4,1)}), s8[4194304]{0:T(1024)(128)(4,1)S(1)}, s32[]{:S(2)}) async-start(s8[4718592]{0:T(1024)(128)(4,1)} %bitcast.81), calls=%async_computation.4 | async-start | bytes 8388608
  215.0 4.6 %slice-start.1 = ((s8[4718592]{0:T(1024)(128)(4,1)}), s8[524288]{0:T(1024)(128)(4,1)S(1)}, s32[]{:S(2)}) async-start(s8[4718592]{0:T(1024)(128)(4,1)} %bitcast.81), calls=%async_computation.5 | async-start | bytes 1048576
  221.5 3.4 %copy-start.8 = (bf16[256,2,128]{2,1,0:T(2,128)(2,1)S(1)}, bf16[256,2,128]{2,1,0:T(2,128)(2,1)}, u32[]{:S(2)}) copy-start(bf16[256,2,128]{2,1,0:T(2,128)(2,1)} %get-tuple-element.15) | copy-start | bytes 393220
  241.0 3.4 %copy-start.4 = (bf16[2304,2,128]{2,1,0:T(2,128)(2,1)S(1)}, bf16[2304,2,128]{2,1,0:T(2,128)(2,1)}, u32[]{:S(2)}) copy-start(bf16[2304,2,128]{2,1,0:T(2,128)(2,1)} %get-tuple-element.14) | copy-start | bytes 3538948
  246.1 1.8 copy-start.6
  246.1 1.8 copy-start.7
where the time goes:
time: 259 us; the launch traced here: 258 us
  waiting for transfers between devices  159 us (61%)
  local copies, waits for them, and re-layouts  34.7 us (13%)
  starting transfers between devices  20.4 us (8%)
  blocking collectives  19.7 us (8%)
  matrix products  13.9 us (5%)
  other arithmetic  10.1 us (4%)
    all_to_all x1, waiting for transfers between devices, body(): lax.all_to_all(to_blocks(queries), 'spatial', split_axis=0, concat_axis=0...  130 us
    ppermute x2, waiting for transfers between devices, with_halo(): before = lax.ppermute(last, axis, up)  18.3 us
    all_to_all x1, blocking collectives, body(): lax.all_to_all(to_blocks(values), 'spatial', split_axis=0, concat_axis=0,...  10.2 us
    all_to_all x1, blocking collectives, body(): lax.all_to_all(result, 'spatial', split_axis=0, concat_axis=0, tiled=True)  9.53 us
    dot_general x4, matrix products, attend(): jnp.einsum('qhd,khd->hqk', query_part, key_part, preferred_element_type=j...  8.18 us
    ppermute x2, starting transfers between devices, with_halo(): before = lax.ppermute(last, axis, up)  6.96 us
    all_to_all x1, waiting for transfers between devices, body(): lax.all_to_all(to_blocks(keys), 'spatial', split_axis=0, concat_axis=0, t...  6.94 us
    concatenate x2, other arithmetic, with_halo(): array = jnp.concatenate([before, array, after], axis=dim)  6.68 us
  transfers between devices with their start and end apart: 6, of which 4 were waited for; matrix products, arithmetic and copies ran while one was open for 2% of the time, Pallas kernels for 0%

commit v1 on v0

--- a/solution.py
+++ b/solution.py
@@ -1,14 +1,18 @@
+import functools
 import math
 
 import jax
 import jax.numpy as jnp
 from jax import lax
+from jax.experimental import pallas as pl
+from jax.experimental.pallas import tpu as pltpu
 from jax.sharding import PartitionSpec as P
 
 D_HEAD = 128
 TILE_T = 4
 TILE_H = 8
 TILE_W = 8
+MESH = pl.DeviceIdType.MESH
 
 
 def with_halo(array, sides, width):
@@ -62,7 +66,7 @@
     return jnp.concatenate(pieces, axis=1)
 
 
-def body(queries, keys, values, window):
+def gathered(queries, keys, values, window):
     space_count = lax.axis_size("spatial")
     time_count = lax.axis_size("temporal")
     tokens_dev, channels = queries.shape
@@ -120,6 +124,282 @@
     return jnp.transpose(shaped, (2, 1, 3, 0, 4)).reshape(tokens_dev, channels)
 
 
+def flipped(index, bits):
+    bit = 1
+    while bit <= bits:
+        if bits & bit:
+            index = index + bit - 2 * bit * ((index // bit) % 2)
+        bit *= 2
+    return index
+
+
+def by_tiles(rows, count):
+    width = count * TILE_W
+    whole = rows.astype(jnp.float32)
+    lines = whole.shape[0] // width
+    return [
+        jnp.concatenate(
+            [whole[r * width + w * TILE_W : r * width + (w + 1) * TILE_W] for r in range(lines)],
+            axis=0,
+        ).astype(rows.dtype)
+        for w in range(count)
+    ]
+
+
+def by_rows(parts):
+    parts = [part.astype(jnp.float32) for part in parts]
+    lines = parts[0].shape[0] // TILE_W
+    return jnp.concatenate(
+        [part[r * TILE_W : (r + 1) * TILE_W] for r in range(lines) for part in parts], axis=0
+    ).astype(jnp.bfloat16)
+
+
+def fused_kernel(
+    times, count, own_heads,
+    q_ref, k_ref, v_ref, win_ref, out_ref,
+    stage_kv, stage_q, kv, qs, outs, arrived, win,
+    kv_send, kv_recv, q_send, q_recv, z_send, z_recv, o_send, o_recv, w_send, w_recv,
+):
+    t = lax.axis_index("temporal")
+    me = lax.axis_index("spatial")
+    part = q_ref.shape[0] // count
+    peers = range(1, count)
+    peer = [flipped(me, d) for d in range(count)]
+
+    def rows_of(index):
+        return pl.ds(pl.multiple_of(index * part, part), part)
+
+    def columns_of(index, h):
+        return pl.ds(pl.multiple_of((index * own_heads + h) * D_HEAD, D_HEAD), D_HEAD)
+
+    def to(d):
+        return {"spatial": peer[d]}
+
+    def kv_copy(d, h, rows):
+        return pltpu.make_async_remote_copy(
+            src_ref=stage_kv.at[d - 1, h],
+            dst_ref=kv.at[1, h, :, :, rows],
+            send_sem=kv_send.at[d - 1, h],
+            recv_sem=kv_recv.at[d - 1, h],
+            device_id=to(d), device_id_type=MESH,
+        )
+
+    def q_copy(d, h, rows):
+        return pltpu.make_async_remote_copy(
+            src_ref=stage_q.at[d - 1, h],
+            dst_ref=qs.at[h, :, rows],
+            send_sem=q_send.at[d - 1, h],
+            recv_sem=q_recv.at[d - 1, h],
+            device_id=to(d), device_id_type=MESH,
+        )
+
+    def w_copy(d, slot):
+        return pltpu.make_async_remote_copy(
+            src_ref=win.at[slot],
+            dst_ref=win.at[slot],
+            send_sem=w_send.at[d - 1],
+            recv_sem=w_recv.at[d - 1],
+            device_id=to(d), device_id_type=MESH,
+        )
+
+    def z_copy(side, d, h):
+        rows = rows_of(peer[d])
+        return pltpu.make_async_remote_copy(
+            src_ref=kv.at[1, h, :, :, rows],
+            dst_ref=kv.at[2 * side, h, :, :, rows],
+            send_sem=z_send.at[side, d, h],
+            recv_sem=z_recv.at[side, d, h],
+            device_id={"temporal": t + 1 - 2 * side}, device_id_type=MESH,
+        )
+
+    def o_copy(d, h, w):
+        return pltpu.make_async_remote_copy(
+            src_ref=outs.at[h, w, rows_of(peer[d])],
+            dst_ref=arrived.at[d - 1, h, w],
+            send_sem=o_send.at[d - 1, h, w],
+            recv_sem=o_recv.at[d - 1, h, w],
+            device_id=to(d), device_id_type=MESH,
+        )
+
+    can_send = (t < times - 1, t > 0)
+    can_take = (t > 0, t < times - 1)
+
+    barrier = pltpu.get_barrier_semaphore()
+    for d in peers:
+        pl.semaphore_signal(barrier, inc=1, device_id=to(d), device_id_type=MESH)
+    for side in range(2):
+        @pl.when(can_send[side])
+        def _(side=side):
+            pl.semaphore_signal(
+                barrier, inc=1, device_id={"temporal": t + 1 - 2 * side}, device_id_type=MESH
+            )
+
+    def lay_kv(d, h):
+        for i, ref in enumerate((k_ref, v_ref)):
+            for w, piece in enumerate(by_tiles(ref[:, columns_of(peer[d], h)], count)):
+                if d:
+                    stage_kv[d - 1, h, i, w] = piece
+                else:
+                    kv[1, h, i, w, rows_of(me)] = piece
+
+    def lay_q(d, h):
+        for w, piece in enumerate(by_tiles(q_ref[:, columns_of(peer[d], h)], count)):
+            if d:
+                stage_q[d - 1, h, w] = piece
+            else:
+                qs[h, w, rows_of(me)] = piece
+
+    def forward(d, h):
+        for side in range(2):
+            @pl.when(can_send[side])
+            def _(side=side):
+                z_copy(side, d, h).start()
+
+    lay_kv(0, 0)
+    win[me] = jnp.zeros(win.shape[1:], win.dtype)
+    win[me, 0:1, 0 : win_ref.shape[1]] = win_ref[...]
+    for side in range(2):
+        @pl.when(jnp.logical_not(can_take[side]))
+        def _(side=side):
+            kv[2 * side] = jnp.zeros(kv.shape[1:], kv.dtype)
+
+    linked = can_send[0].astype(jnp.int32) + can_send[1].astype(jnp.int32)
+    pl.semaphore_wait(barrier, count - 1 + linked)
+
+    for h in range(own_heads):
+        if h:
+            lay_kv(0, h)
+        forward(0, h)
+        for d in peers:
+            lay_kv(d, h)
+            kv_copy(d, h, rows_of(me)).start()
+    for d in peers:
+        w_copy(d, me).start()
+    for h in range(own_heads):
+        for d in peers:
+            lay_q(d, h)
+            q_copy(d, h, rows_of(me)).start()
+        lay_q(0, h)
+
+    for h in range(own_heads):
+        for d in peers:
+            kv_copy(d, h, rows_of(peer[d])).wait_recv()
+            forward(d, h)
+    for d in peers:
+        w_copy(d, peer[d]).wait_recv()
+
+    factor = math.log2(math.e) / math.sqrt(D_HEAD)
+    for h in range(own_heads):
+        for d in peers:
+            q_copy(d, h, rows_of(peer[d])).wait_recv()
+        for side in range(2):
+            @pl.when(can_take[side])
+            def _(side=side):
+                for d in range(count):
+                    z_copy(side, d, h).wait_recv()
+        for w in range(count):
+            low, high = max(w - 1, 0), min(w + 2, count)
+            query = qs[h, w]
+            pattern = win[w, 0:1, :]
+            scores, limits = [], []
+            for p in range(3):
+                for c in range(low, high):
+                    scores.append(lax.dot_general(
+                        query, kv[p, h, 0, c], (((1,), (1,)), ((), ())),
+                        preferred_element_type=jnp.float32,
+                    ))
+                    entry = 9 * p + 3 + (c - w + 1)
+                    ok = pattern[:, entry : entry + 1] == 1
+                    if p != 1:
+                        ok = jnp.logical_and(ok, can_take[p // 2])
+                    limits.append(jnp.where(ok, 0.0, jnp.inf).astype(jnp.float32))
+            peak = None
+            for score, limit in zip(scores, limits):
+                top = jnp.max(score, axis=1, keepdims=True) - limit
+                peak = top if peak is None else jnp.maximum(peak, top)
+            total, mixed = None, None
+            for i, (score, limit) in enumerate(zip(scores, limits)):
+                p, c = i // (high - low), low + i % (high - low)
+                weights = jnp.exp2((score - (peak + limit)) * factor)
+                part_total = jnp.sum(weights, axis=1, keepdims=True)
+                part_mixed = jnp.dot(
+                    weights.astype(jnp.bfloat16), kv[p, h, 1, c],
+                    preferred_element_type=jnp.float32,
+                )
+                total = part_total if total is None else total + part_total
+                mixed = part_mixed if mixed is None else mixed + part_mixed
+            outs[h, w] = (mixed / total).astype(jnp.bfloat16)
+            for d in peers:
+                o_copy(d, h, w).start()
+
+    for h in range(own_heads):
+        out_ref[:, columns_of(me, h)] = by_rows([outs[h, w, rows_of(me)] for w in range(count)])
+        for d in peers:
+            for w in range(count):
+                o_copy(d, h, w).wait_recv()
+            out_ref[:, columns_of(peer[d], h)] = by_rows([arrived[d - 1, h, w] for w in range(count)])
+
+    for h in range(own_heads):
+        for d in peers:
+            kv_copy(d, h, rows_of(me)).wait_send()
+            q_copy(d, h, rows_of(me)).wait_send()
+            for w in range(count):
+                o_copy(d, h, w).wait_send()
+        for side in range(2):
+            @pl.when(can_send[side])
+            def _(side=side):
+                for d in range(count):
+                    z_copy(side, d, h).wait_send()
+    for d in peers:
+        w_copy(d, me).wait_send()
+
+
+def fused(queries, keys, values, window):
+    count, times = lax.axis_size("spatial"), lax.axis_size("temporal")
+    tokens, channels = queries.shape
+    own = channels // (D_HEAD * count)
+    part = tokens // count
+    vmem = pl.BlockSpec(memory_space=pltpu.VMEM)
+    dma = pltpu.SemaphoreType.DMA
+    pairs = own * count * (3 * count - 2) * 3 * tokens * tokens * D_HEAD
+    return pl.pallas_call(
+        functools.partial(fused_kernel, times, count, own),
+        out_shape=jax.ShapeDtypeStruct(queries.shape, queries.dtype),
+        in_specs=[vmem] * 4,
+        out_specs=vmem,
+        scratch_shapes=[
+            pltpu.VMEM((count - 1, own, 2, count, part, D_HEAD), jnp.bfloat16),
+            pltpu.VMEM((count - 1, own, count, part, D_HEAD), jnp.bfloat16),
+            pltpu.VMEM((3, own, 2, count, tokens, D_HEAD), jnp.bfloat16),
+            pltpu.VMEM((own, count, tokens, D_HEAD), jnp.bfloat16),
+            pltpu.VMEM((own, count, tokens, D_HEAD), jnp.bfloat16),
+            pltpu.VMEM((count - 1, own, count, part, D_HEAD), jnp.bfloat16),
+            pltpu.VMEM((count, 8, 128), jnp.int32),
+            dma((count - 1, own)), dma((count - 1, own)),
+            dma((count - 1, own)), dma((count - 1, own)),
+            dma((2, count, own)), dma((2, count, own)),
+            dma((count - 1, own, count)), dma((count - 1, own, count)),
+            dma((count - 1,)), dma((count - 1,)),
+        ],
+        compiler_params=pltpu.CompilerParams(
+            collective_id=0, has_side_effects=True, vmem_limit_bytes=48 * 2**20
+        ),
+        cost_estimate=pl.CostEstimate(
+            flops=4 * pairs, bytes_accessed=4 * tokens * channels * 2, transcendentals=pairs // D_HEAD
+        ),
+    )(queries, keys, values, window.reshape(1, -1))
+
+
+def body(queries, keys, values, window):
+    count = lax.axis_size("spatial")
+    tokens, channels = queries.shape
+    heads_here = channels // D_HEAD
+    whole_tiles = window.shape[1] == 1 and window.shape[2] == 1 and tokens == TILE_T * TILE_H * TILE_W
+    if whole_tiles and count & (count - 1) == 0 and heads_here % count == 0:
+        return fused(queries, keys, values, window)
+    return gathered(queries, keys, values, window)
+
+
 def solution(mesh):
     return jax.shard_map(
         body,

time: 259 us -> 52.8 us (0.20)
  waiting for transfers between devices: 159 us -> 0 us
  Pallas kernels: 0 us -> 48 us
  local copies, waits for them, and re-layouts: 34.7 us -> 4.57 us
  starting transfers between devices: 20.4 us -> 0 us
  blocking collectives: 19.7 us -> 0 us
  matrix products: 13.9 us -> 0 us
  other arithmetic: 10.1 us -> 0 us
    all_to_all x2 -> x0, waiting for transfers between devices: 137 us -> none  [the longest x1 130 us: body(): lax.all_to_all(to_blocks(queries), 'spatial', split_axis=0, concat_axis=0...]
    pallas_call x0 -> x1, Pallas kernels: none -> 48 us  [fused(): pl.pallas_call(functools.partial(fused_kernel, times, count, own), out_sh...]
    ppermute x4 -> x0, waiting for transfers between devices: 22.5 us -> none  [the longest x2 18.3 us: with_halo(): before = lax.ppermute(last, axis, up)]
    all_to_all x2 -> x0, blocking collectives: 19.7 us -> none  [the longest x1 10.2 us: body(): lax.all_to_all(to_blocks(values), 'spatial', split_axis=0, concat_axis=0,...]
    slice x6 -> x0, local copies, waits for them, and re-layouts: 17.4 us -> none  [the longest x2 5.43 us: body(): padded[1, :, :, row_low:row_high, 0:3].reshape(-1, heads_here, D_HEAD)]
    dot_general x8 -> x0, matrix products: 13.9 us -> none  [the longest x4 8.18 us: attend(): jnp.einsum('qhd,khd->hqk', query_part, key_part, preferred_element_type=j...]
    all_to_all x2 -> x0, starting transfers between devices: 10.8 us -> none  [the longest x1 5.68 us: body(): lax.all_to_all(to_blocks(queries), 'spatial', split_axis=0, concat_axis=0...]
    ppermute x4 -> x0, starting transfers between devices: 9.55 us -> none  [the longest x2 6.96 us: with_halo(): before = lax.ppermute(last, axis, up)]
  transfers between devices with their start and end apart: 6 -> 0, of which waited for: 4 -> 0; matrix products, arithmetic and copies ran while one was open for 2% -> 0% of each run, Pallas kernels for 0% -> 0%
where the time goes in v1:
time: 52.8 us; the launch traced here: 52.6 us
  Pallas kernels  48 us (91%)
  local copies, waits for them, and re-layouts  4.57 us (9%)
    pallas_call x1, Pallas kernels, fused(): pl.pallas_call(functools.partial(fused_kernel, times, count, own), out_sh...  48 us
    unnamed x9, local copies, waits for them, and re-layouts  4.57 us

profile of v1, /device:TPU:0, one launch (start us, length us, event | category | flops | bytes accessed | tf_op | source)
XLA Modules:
  0.0 52.6 jit_solution(4882439064303002376)
XLA Ops:
  0.0 0.0 copy-start.3
  0.0 0.7 %copy-done.3 = s32[1,1,1,27]{3,2,1,0:T(1,128)S(1)} copy-done((s32[1,1,1,27]{3,2,1,0:T(1,128)S(1)}, s32[1,1,1,27]{3,2,1,0:T(1,128)}, u32[]{:S(2)}) %copy-start.3) | copy-done | bytes 132
  0.7 0.0 copy-start
  0.7 1.0 %copy-done = bf16[256,1024]{1,0:T(8,128)(2,1)S(1)} copy-done((bf16[256,1024]{1,0:T(8,128)(2,1)S(1)}, bf16[256,1024]{1,0:T(8,128)(2,1)}, u32[]{:S(2)}) %copy-start) | copy-done | bytes 524312
  1.7 0.0 copy-start.1
  1.7 1.0 %copy-done.1 = bf16[256,1024]{1,0:T(8,128)(2,1)S(1)} copy-done((bf16[256,1024]{1,0:T(8,128)(2,1)S(1)}, bf16[256,1024]{1,0:T(8,128)(2,1)}, u32[]{:S(2)}) %copy-start.1) | copy-done | bytes 524312
  2.7 0.0 copy-start.2
  2.7 1.0 %copy-done.2 = bf16[256,1024]{1,0:T(8,128)(2,1)S(1)} copy-done((bf16[256,1024]{1,0:T(8,128)(2,1)S(1)}, bf16[256,1024]{1,0:T(8,128)(2,1)}, u32[]{:S(2)}) %copy-start.2) | copy-done | bytes 524312
  3.8 48.0 %shard_map.46 = bf16[256,1024]{1,0:T(8,128)(2,1)S(1)} custom-call(bf16[256,1024]{1,0:T(8,128)(2,1)S(1)} %copy-done, bf16[256,1024]{1,0:T(8,128)(2,1)S(1)} %copy-done.1, bf16[256,1024]{1,0:T(8,128)(2,1)S(1)} %copy-done.2, s32[1,27]{1,0:T(1,128)S(1)} %bitcast.1), custom_call_target="tpu_custom_call" | custom-call | flops 8053063680 | bytes 2097152 | tf_op jit(solution)/shard_map/pallas_call | solution.py:365
  51.8 0.8 %copy.6 = bf16[256,1024]{1,0:T(8,128)(2,1)} copy(bf16[256,1024]{1,0:T(8,128)(2,1)S(1)} %shard_map.46) | data formatting | bytes 1048576
Async XLA Ops:
  0.0 0.7 %copy-start.3 = (s32[1,1,1,27]{3,2,1,0:T(1,128)S(1)}, s32[1,1,1,27]{3,2,1,0:T(1,128)}, u32[]{:S(2)}) copy-start(s32[1,1,1,27]{3,2,1,0:T(1,128)} %param.7) | copy-start | bytes 328
  0.7 1.0 %copy-start = (bf16[256,1024]{1,0:T(8,128)(2,1)S(1)}, bf16[256,1024]{1,0:T(8,128)(2,1)}, u32[]{:S(2)}) copy-start(bf16[256,1024]{1,0:T(8,128)(2,1)} %q_ref.1) | copy-start | bytes 1572868
  1.7 1.0 %copy-start.1 = (bf16[256,1024]{1,0:T(8,128)(2,1)S(1)}, bf16[256,1024]{1,0:T(8,128)(2,1)}, u32[]{:S(2)}) copy-start(bf16[256,1024]{1,0:T(8,128)(2,1)} %k_ref.1) | copy-start | bytes 1572868
  2.7 1.0 %copy-start.2 = (bf16[256,1024]{1,0:T(8,128)(2,1)S(1)}, bf16[256,1024]{1,0:T(8,128)(2,1)}, u32[]{:S(2)}) copy-start(bf16[256,1024]{1,0:T(8,128)(2,1)} %v_ref.1) | copy-start | bytes 1572868

commit v2 on v1

--- a/solution.py
+++ b/solution.py
@@ -12,6 +12,7 @@
 TILE_T = 4
 TILE_H = 8
 TILE_W = 8
+LANES = 128
 MESH = pl.DeviceIdType.MESH
 
 
@@ -156,9 +157,10 @@
 
 def fused_kernel(
     times, count, own_heads,
-    q_ref, k_ref, v_ref, win_ref, out_ref,
-    stage_kv, stage_q, kv, qs, outs, arrived, win,
+    q_hbm, k_hbm, v_hbm, win_hbm, out_ref,
+    q_ref, k_ref, v_ref, win_ref, stage_kv, stage_q, kv, qs, outs, arrived, win,
     kv_send, kv_recv, q_send, q_recv, z_send, z_recv, o_send, o_recv, w_send, w_recv,
+    in_sem, win_sem,
 ):
     t = lax.axis_index("temporal")
     me = lax.axis_index("spatial")
@@ -220,6 +222,24 @@
             recv_sem=o_recv.at[d - 1, h, w],
             device_id=to(d), device_id_type=MESH,
         )
+
+    def in_copy(i, d, h):
+        here = columns_of(peer[d], h)
+        return pltpu.make_async_copy(
+            (k_hbm, v_hbm, q_hbm)[i].at[:, here],
+            (k_ref, v_ref, q_ref)[i].at[:, here],
+            in_sem.at[i, d, h],
+        )
+
+    for h in range(own_heads):
+        for d in range(count):
+            for i in range(2):
+                in_copy(i, d, h).start()
+    win_copy = pltpu.make_async_copy(win_hbm, win_ref, win_sem)
+    win_copy.start()
+    for h in range(own_heads):
+        for d in range(count):
+            in_copy(2, d, h).start()
 
     can_send = (t < times - 1, t > 0)
     can_take = (t > 0, t < times - 1)
@@ -236,6 +256,7 @@
 
     def lay_kv(d, h):
         for i, ref in enumerate((k_ref, v_ref)):
+            in_copy(i, d, h).wait()
             for w, piece in enumerate(by_tiles(ref[:, columns_of(peer[d], h)], count)):
                 if d:
                     stage_kv[d - 1, h, i, w] = piece
@@ -243,6 +264,7 @@
                     kv[1, h, i, w, rows_of(me)] = piece
 
     def lay_q(d, h):
+        in_copy(2, d, h).wait()
         for w, piece in enumerate(by_tiles(q_ref[:, columns_of(peer[d], h)], count)):
             if d:
                 stage_q[d - 1, h, w] = piece
@@ -256,6 +278,7 @@
                 z_copy(side, d, h).start()
 
     lay_kv(0, 0)
+    win_copy.wait()
     win[me] = jnp.zeros(win.shape[1:], win.dtype)
     win[me, 0:1, 0 : win_ref.shape[1]] = win_ref[...]
     for side in range(2):
@@ -301,33 +324,41 @@
             low, high = max(w - 1, 0), min(w + 2, count)
             query = qs[h, w]
             pattern = win[w, 0:1, :]
-            scores, limits = [], []
-            for p in range(3):
-                for c in range(low, high):
-                    scores.append(lax.dot_general(
-                        query, kv[p, h, 0, c], (((1,), (1,)), ((), ())),
-                        preferred_element_type=jnp.float32,
-                    ))
-                    entry = 9 * p + 3 + (c - w + 1)
-                    ok = pattern[:, entry : entry + 1] == 1
-                    if p != 1:
-                        ok = jnp.logical_and(ok, can_take[p // 2])
-                    limits.append(jnp.where(ok, 0.0, jnp.inf).astype(jnp.float32))
-            peak = None
-            for score, limit in zip(scores, limits):
-                top = jnp.max(score, axis=1, keepdims=True) - limit
+            wide = high - low
+            keys = kv[:, h, 0, low:high].reshape(-1, D_HEAD)
+            scores = lax.dot_general(
+                query, keys, (((1,), (1,)), ((), ())), preferred_element_type=jnp.float32
+            )
+            blocks, limits, peak = [], [], None
+            for i in range(3 * wide):
+                p, c = i // wide, low + i % wide
+                start = i * query.shape[0]
+                halves = [
+                    scores[:, j : j + LANES] for j in range(start, start + query.shape[0], LANES)
+                ]
+                entry = 9 * p + 3 + (c - w + 1)
+                ok = pattern[:, entry : entry + 1] == 1
+                if p != 1:
+                    ok = jnp.logical_and(ok, can_take[p // 2])
+                limit = jnp.where(ok, 0.0, jnp.inf).astype(jnp.float32)
+                top = functools.reduce(jnp.maximum, halves) - limit
                 peak = top if peak is None else jnp.maximum(peak, top)
-            total, mixed = None, None
-            for i, (score, limit) in enumerate(zip(scores, limits)):
-                p, c = i // (high - low), low + i % (high - low)
-                weights = jnp.exp2((score - (peak + limit)) * factor)
-                part_total = jnp.sum(weights, axis=1, keepdims=True)
-                part_mixed = jnp.dot(
-                    weights.astype(jnp.bfloat16), kv[p, h, 1, c],
-                    preferred_element_type=jnp.float32,
-                )
-                total = part_total if total is None else total + part_total
-                mixed = part_mixed if mixed is None else mixed + part_mixed
+                blocks.append(halves)
+                limits.append(limit)
+            peak = jnp.broadcast_to(jnp.max(peak, axis=1, keepdims=True), peak.shape)
+            total, rounded = None, []
+            for halves, limit in zip(blocks, limits):
+                base = peak + limit
+                for half in halves:
+                    weights = jnp.exp2((half - base) * factor)
+                    total = weights if total is None else total + weights
+                    rounded.append(weights.astype(jnp.bfloat16))
+            total = jnp.sum(total, axis=1, keepdims=True)
+            mixed = jnp.dot(
+                jnp.concatenate(rounded, axis=1),
+                kv[:, h, 1, low:high].reshape(-1, D_HEAD),
+                preferred_element_type=jnp.float32,
+            )
             outs[h, w] = (mixed / total).astype(jnp.bfloat16)
             for d in peers:
                 o_copy(d, h, w).start()
@@ -365,9 +396,13 @@
     return pl.pallas_call(
         functools.partial(fused_kernel, times, count, own),
         out_shape=jax.ShapeDtypeStruct(queries.shape, queries.dtype),
-        in_specs=[vmem] * 4,
+        in_specs=[pl.BlockSpec(memory_space=pl.ANY)] * 4,
         out_specs=vmem,
         scratch_shapes=[
+            pltpu.VMEM(queries.shape, jnp.bfloat16),
+            pltpu.VMEM(queries.shape, jnp.bfloat16),
+            pltpu.VMEM(queries.shape, jnp.bfloat16),
+            pltpu.VMEM((1, window.size), jnp.int32),
             pltpu.VMEM((count - 1, own, 2, count, part, D_HEAD), jnp.bfloat16),
             pltpu.VMEM((count - 1, own, count, part, D_HEAD), jnp.bfloat16),
             pltpu.VMEM((3, own, 2, count, tokens, D_HEAD), jnp.bfloat16),
@@ -380,9 +415,10 @@
             dma((2, count, own)), dma((2, count, own)),
             dma((count - 1, own, count)), dma((count - 1, own, count)),
             dma((count - 1,)), dma((count - 1,)),
+            dma((3, count, own)), dma,
         ],
         compiler_params=pltpu.CompilerParams(
-            collective_id=0, has_side_effects=True, vmem_limit_bytes=48 * 2**20
+            collective_id=0, has_side_effects=True, vmem_limit_bytes=60 * 2**20
         ),
         cost_estimate=pl.CostEstimate(
             flops=4 * pairs, bytes_accessed=4 * tokens * channels * 2, transcendentals=pairs // D_HEAD

time: 52.8 us -> 40.5 us (0.77)
  Pallas kernels: 48 us -> 38.4 us
  local copies, waits for them, and re-layouts: 4.57 us -> 1.87 us
    pallas_call x1, Pallas kernels: 48 us -> 38.4 us  [fused(): pl.pallas_call(functools.partial(fused_kernel, times, count, own), out_sh...]
    unnamed x9 -> x1, local copies, waits for them, and re-layouts: 4.57 us -> 1.87 us
where the time goes in v2:
time: 40.5 us; the launch traced here: 40.3 us
  Pallas kernels  38.4 us (95%)
  local copies, waits for them, and re-layouts  1.87 us (5%)
    pallas_call x1, Pallas kernels, fused(): pl.pallas_call(functools.partial(fused_kernel, times, count, own), out_sh...  38.4 us
    unnamed x1, local copies, waits for them, and re-layouts  1.87 us

profile of v2, /device:TPU:0, one launch (start us, length us, event | category | flops | bytes accessed | tf_op | source)
XLA Modules:
  0.0 40.3 jit_solution(16302844189974467028)
XLA Ops:
  0.0 38.4 %shard_map.46 = bf16[256,1024]{1,0:T(8,128)(2,1)} custom-call(bf16[256,1024]{1,0:T(8,128)(2,1)} %q_hbm.1, bf16[256,1024]{1,0:T(8,128)(2,1)} %k_hbm.1, bf16[256,1024]{1,0:T(8,128)(2,1)} %v_hbm.1, s32[1,27]{1,0:T(1,128)} %bitcast.1), custom_call_target="tpu_custom_call" | custom-call | flops 8053063680 | bytes 2097152 | tf_op jit(solution)/shard_map/pallas_call | solution.py:396
  38.4 1.9 %copy.6 = bf16[256,1024]{1,0:T(8,128)(2,1)} copy(bf16[256,1024]{1,0:T(8,128)(2,1)} %shard_map.46) | data formatting | bytes 1048576

commit v3 on v2

--- a/solution.py
+++ b/solution.py
@@ -289,25 +289,33 @@
     linked = can_send[0].astype(jnp.int32) + can_send[1].astype(jnp.int32)
     pl.semaphore_wait(barrier, count - 1 + linked)
 
-    for h in range(own_heads):
-        if h:
-            lay_kv(0, h)
-        forward(0, h)
-        for d in peers:
-            lay_kv(d, h)
-            kv_copy(d, h, rows_of(me)).start()
+    def early(d, h):
+        return h == 0 or (h == 1 and d <= 1)
+
+    forward(0, 0)
+    for d in peers:
+        lay_kv(d, 0)
+        kv_copy(d, 0, rows_of(me)).start()
     for d in peers:
         w_copy(d, me).start()
-    for h in range(own_heads):
-        for d in peers:
+    for h in range(1, own_heads):
+        for d in range(count):
+            lay_kv(d, h)
+            if d == 0 and early(d, h):
+                forward(d, h)
+    for h in range(own_heads):
+        for d in range(count):
             lay_q(d, h)
-            q_copy(d, h, rows_of(me)).start()
-        lay_q(0, h)
 
     for h in range(own_heads):
         for d in peers:
             kv_copy(d, h, rows_of(peer[d])).wait_recv()
-            forward(d, h)
+            if early(d, h):
+                forward(d, h)
+            if h + 1 < own_heads:
+                kv_copy(d, h + 1, rows_of(me)).start()
+            else:
+                q_copy(d, 0, rows_of(me)).start()
     for d in peers:
         w_copy(d, peer[d]).wait_recv()
 
@@ -315,11 +323,17 @@
     for h in range(own_heads):
         for d in peers:
             q_copy(d, h, rows_of(peer[d])).wait_recv()
+            if h + 1 < own_heads:
+                q_copy(d, h + 1, rows_of(me)).start()
         for side in range(2):
             @pl.when(can_take[side])
             def _(side=side):
                 for d in range(count):
                     z_copy(side, d, h).wait_recv()
+        if h + 1 < own_heads:
+            for d in range(count):
+                if not early(d, h + 1):
+                    forward(d, h + 1)
         for w in range(count):
             low, high = max(w - 1, 0), min(w + 2, count)
             query = qs[h, w]

time: 40.5 us -> 40.5 us (level)
  no operation moved by 1% of the time
where the time goes in v3:
time: 40.5 us; the launch traced here: 40.2 us
  Pallas kernels  38.4 us (95%)
  local copies, waits for them, and re-layouts  1.87 us (5%)
    pallas_call x1, Pallas kernels, fused(): pl.pallas_call(functools.partial(fused_kernel, times, count, own), out_sh...  38.4 us
    unnamed x1, local copies, waits for them, and re-layouts  1.87 us

profile of v3, /device:TPU:0, one launch (start us, length us, event | category | flops | bytes accessed | tf_op | source)
XLA Modules:
  0.0 40.2 jit_solution(15165909056595096695)
XLA Ops:
  0.0 38.4 %shard_map.46 = bf16[256,1024]{1,0:T(8,128)(2,1)} custom-call(bf16[256,1024]{1,0:T(8,128)(2,1)} %q_hbm.1, bf16[256,1024]{1,0:T(8,128)(2,1)} %k_hbm.1, bf16[256,1024]{1,0:T(8,128)(2,1)} %v_hbm.1, s32[1,27]{1,0:T(1,128)} %bitcast.1), custom_call_target="tpu_custom_call" | custom-call | flops 8053063680 | bytes 2097152 | tf_op jit(solution)/shard_map/pallas_call | solution.py:410
  38.4 1.9 %copy.6 = bf16[256,1024]{1,0:T(8,128)(2,1)} copy(bf16[256,1024]{1,0:T(8,128)(2,1)} %shard_map.46) | data formatting | bytes 1048576

commit v4 on v3

--- a/solution.py
+++ b/solution.py
@@ -155,6 +155,11 @@
     ).astype(jnp.bfloat16)
 
 
+def column_groups(count):
+    first = min(2, count)
+    return [(0, first)] + [(c, 1) for c in range(first, count)]
+
+
 def fused_kernel(
     times, count, own_heads,
     q_hbm, k_hbm, v_hbm, win_hbm, out_ref,
@@ -166,6 +171,7 @@
     me = lax.axis_index("spatial")
     part = q_ref.shape[0] // count
     peers = range(1, count)
+    groups = column_groups(count)
     peer = [flipped(me, d) for d in range(count)]
 
     def rows_of(index):
@@ -204,13 +210,13 @@
             device_id=to(d), device_id_type=MESH,
         )
 
-    def z_copy(side, d, h):
-        rows = rows_of(peer[d])
+    def z_copy(side, d, h, j):
+        rows, tiles = rows_of(peer[d]), pl.ds(*groups[j])
         return pltpu.make_async_remote_copy(
-            src_ref=kv.at[1, h, :, :, rows],
-            dst_ref=kv.at[2 * side, h, :, :, rows],
-            send_sem=z_send.at[side, d, h],
-            recv_sem=z_recv.at[side, d, h],
+            src_ref=kv.at[1, h, :, tiles, rows],
+            dst_ref=kv.at[2 * side, h, :, tiles, rows],
+            send_sem=z_send.at[side, d, h, j],
+            recv_sem=z_recv.at[side, d, h, j],
             device_id={"temporal": t + 1 - 2 * side}, device_id_type=MESH,
         )
 
@@ -271,11 +277,14 @@
             else:
                 qs[h, w, rows_of(me)] = piece
 
-    def forward(d, h):
+    def forward(d, h, these):
         for side in range(2):
             @pl.when(can_send[side])
             def _(side=side):
-                z_copy(side, d, h).start()
+                for j in these:
+                    z_copy(side, d, h, j).start()
+
+    every = range(len(groups))
 
     lay_kv(0, 0)
     win_copy.wait()
@@ -292,7 +301,7 @@
     def early(d, h):
         return h == 0 or (h == 1 and d <= 1)
 
-    forward(0, 0)
+    forward(0, 0, every)
     for d in peers:
         lay_kv(d, 0)
         kv_copy(d, 0, rows_of(me)).start()
@@ -302,7 +311,7 @@
         for d in range(count):
             lay_kv(d, h)
             if d == 0 and early(d, h):
-                forward(d, h)
+                forward(d, h, every)
     for h in range(own_heads):
         for d in range(count):
             lay_q(d, h)
@@ -311,7 +320,7 @@
         for d in peers:
             kv_copy(d, h, rows_of(peer[d])).wait_recv()
             if early(d, h):
-                forward(d, h)
+                forward(d, h, every)
             if h + 1 < own_heads:
                 kv_copy(d, h + 1, rows_of(me)).start()
             else:
@@ -319,22 +328,36 @@
     for d in peers:
         w_copy(d, peer[d]).wait_recv()
 
+    def bring_home(h):
+        out_ref[:, columns_of(me, h)] = by_rows([outs[h, w, rows_of(me)] for w in range(count)])
+        for d in peers:
+            for w in range(count):
+                o_copy(d, h, w).wait_recv()
+            out_ref[:, columns_of(peer[d], h)] = by_rows([arrived[d - 1, h, w] for w in range(count)])
+
     factor = math.log2(math.e) / math.sqrt(D_HEAD)
     for h in range(own_heads):
         for d in peers:
             q_copy(d, h, rows_of(peer[d])).wait_recv()
             if h + 1 < own_heads:
                 q_copy(d, h + 1, rows_of(me)).start()
-        for side in range(2):
-            @pl.when(can_take[side])
-            def _(side=side):
-                for d in range(count):
-                    z_copy(side, d, h).wait_recv()
-        if h + 1 < own_heads:
-            for d in range(count):
-                if not early(d, h + 1):
-                    forward(d, h + 1)
         for w in range(count):
+            if w < len(groups):
+                for side in range(2):
+                    @pl.when(can_take[side])
+                    def _(side=side):
+                        for d in range(count):
+                            z_copy(side, d, h, w).wait_recv()
+                if w == len(groups) - 1 and h + 1 < own_heads:
+                    for d in range(count):
+                        if not early(d, h + 1):
+                            forward(d, h + 1, every[:2])
+                if w == 0 and h:
+                    for d in range(count):
+                        if not early(d, h):
+                            forward(d, h, every[2:])
+                if w == len(groups) - 1 and h:
+                    bring_home(h - 1)
             low, high = max(w - 1, 0), min(w + 2, count)
             query = qs[h, w]
             pattern = win[w, 0:1, :]
@@ -377,12 +400,7 @@
             for d in peers:
                 o_copy(d, h, w).start()
 
-    for h in range(own_heads):
-        out_ref[:, columns_of(me, h)] = by_rows([outs[h, w, rows_of(me)] for w in range(count)])
-        for d in peers:
-            for w in range(count):
-                o_copy(d, h, w).wait_recv()
-            out_ref[:, columns_of(peer[d], h)] = by_rows([arrived[d - 1, h, w] for w in range(count)])
+    bring_home(own_heads - 1)
 
     for h in range(own_heads):
         for d in peers:
@@ -394,7 +412,8 @@
             @pl.when(can_send[side])
             def _(side=side):
                 for d in range(count):
-                    z_copy(side, d, h).wait_send()
+                    for j in every:
+                        z_copy(side, d, h, j).wait_send()
     for d in peers:
         w_copy(d, me).wait_send()
 
@@ -404,6 +423,7 @@
     tokens, channels = queries.shape
     own = channels // (D_HEAD * count)
     part = tokens // count
+    groups = len(column_groups(count))
     vmem = pl.BlockSpec(memory_space=pltpu.VMEM)
     dma = pltpu.SemaphoreType.DMA
     pairs = own * count * (3 * count - 2) * 3 * tokens * tokens * D_HEAD
@@ -426,7 +446,7 @@
             pltpu.VMEM((count, 8, 128), jnp.int32),
             dma((count - 1, own)), dma((count - 1, own)),
             dma((count - 1, own)), dma((count - 1, own)),
-            dma((2, count, own)), dma((2, count, own)),
+            dma((2, count, own, groups)), dma((2, count, own, groups)),
             dma((count - 1, own, count)), dma((count - 1, own, count)),
             dma((count - 1,)), dma((count - 1,)),
             dma((3, count, own)), dma,

time: 40.5 us -> 44 us (1.086)
  Pallas kernels: 38.4 us -> 41.9 us
    pallas_call x1, Pallas kernels: 38.4 us -> 41.9 us  [fused(): pl.pallas_call(functools.partial(fused_kernel, times, count, own), out_sh...]
where the time goes in v4:
time: 44 us; the launch traced here: 43.7 us
  Pallas kernels  41.9 us (95%)
  local copies, waits for them, and re-layouts  1.87 us (4%)
    pallas_call x1, Pallas kernels, fused(): pl.pallas_call(functools.partial(fused_kernel, times, count, own), out_sh...  41.9 us
    unnamed x1, local copies, waits for them, and re-layouts  1.87 us

profile of v4, /device:TPU:0, one launch (start us, length us, event | category | flops | bytes accessed | tf_op | source)
XLA Modules:
  0.0 43.7 jit_solution(1080317496429764915)
XLA Ops:
  0.0 41.9 %shard_map.46 = bf16[256,1024]{1,0:T(8,128)(2,1)} custom-call(bf16[256,1024]{1,0:T(8,128)(2,1)} %q_hbm.1, bf16[256,1024]{1,0:T(8,128)(2,1)} %k_hbm.1, bf16[256,1024]{1,0:T(8,128)(2,1)} %v_hbm.1, s32[1,27]{1,0:T(1,128)} %bitcast.1), custom_call_target="tpu_custom_call" | custom-call | flops 8053063680 | bytes 2097152 | tf_op jit(solution)/shard_map/pallas_call | solution.py:430
  41.9 1.9 %copy.6 = bf16[256,1024]{1,0:T(8,128)(2,1)} copy(bf16[256,1024]{1,0:T(8,128)(2,1)} %shard_map.46) | data formatting | bytes 1048576

commit v5 on v3

--- a/solution.py
+++ b/solution.py
@@ -319,12 +319,38 @@
     for d in peers:
         w_copy(d, peer[d]).wait_recv()
 
+    def bring_home(h):
+        out_ref[:, columns_of(me, h)] = by_rows([outs[h, w, rows_of(me)] for w in range(count)])
+        for d in peers:
+            for w in range(count):
+                o_copy(d, h, w).wait_recv()
+            out_ref[:, columns_of(peer[d], h)] = by_rows([arrived[d - 1, h, w] for w in range(count)])
+
+    def limit_of(w, p, c):
+        entry = 9 * p + 3 + (c - w + 1)
+        ok = win[w, 0:1, entry : entry + 1] == 1
+        if p != 1:
+            ok = jnp.logical_and(ok, can_take[p // 2])
+        return jnp.where(ok, 0.0, jnp.inf).astype(jnp.float32)
+
+    def score(h, w, p, c):
+        return lax.dot_general(
+            qs[h, w], kv[p, h, 0, c], (((1,), (1,)), ((), ())), preferred_element_type=jnp.float32
+        )
+
+    def halves_of(block):
+        return [block[:, j : j + LANES] for j in range(0, block.shape[1], LANES)]
+
     factor = math.log2(math.e) / math.sqrt(D_HEAD)
+    near = [range(max(w - 1, 0), min(w + 2, count)) for w in range(count)]
     for h in range(own_heads):
         for d in peers:
             q_copy(d, h, rows_of(peer[d])).wait_recv()
             if h + 1 < own_heads:
                 q_copy(d, h + 1, rows_of(me)).start()
+        scores = [{(1, c): score(h, w, 1, c) for c in near[w]} for w in range(count)]
+        if h:
+            bring_home(h - 1)
         for side in range(2):
             @pl.when(can_take[side])
             def _(side=side):
@@ -334,55 +360,43 @@
             for d in range(count):
                 if not early(d, h + 1):
                     forward(d, h + 1)
+
+        later = [[(p, c) for p in (0, 2) for c in near[w]] for w in range(count)]
+        for spot in later[0]:
+            scores[0][spot] = score(h, 0, *spot)
         for w in range(count):
-            low, high = max(w - 1, 0), min(w + 2, count)
-            query = qs[h, w]
-            pattern = win[w, 0:1, :]
-            wide = high - low
-            keys = kv[:, h, 0, low:high].reshape(-1, D_HEAD)
-            scores = lax.dot_general(
-                query, keys, (((1,), (1,)), ((), ())), preferred_element_type=jnp.float32
-            )
-            blocks, limits, peak = [], [], None
-            for i in range(3 * wide):
-                p, c = i // wide, low + i % wide
-                start = i * query.shape[0]
-                halves = [
-                    scores[:, j : j + LANES] for j in range(start, start + query.shape[0], LANES)
-                ]
-                entry = 9 * p + 3 + (c - w + 1)
-                ok = pattern[:, entry : entry + 1] == 1
-                if p != 1:
-                    ok = jnp.logical_and(ok, can_take[p // 2])
-                limit = jnp.where(ok, 0.0, jnp.inf).astype(jnp.float32)
-                top = functools.reduce(jnp.maximum, halves) - limit
-                peak = top if peak is None else jnp.maximum(peak, top)
-                blocks.append(halves)
-                limits.append(limit)
+            spots = [(p, c) for p in range(3) for c in near[w]]
+            limits = {spot: limit_of(w, *spot) for spot in spots}
+            tops = [
+                functools.reduce(jnp.maximum, halves_of(scores[w][spot])) - limits[spot]
+                for spot in spots
+            ]
+            peak = functools.reduce(jnp.maximum, tops)
             peak = jnp.broadcast_to(jnp.max(peak, axis=1, keepdims=True), peak.shape)
-            total, rounded = None, []
-            for halves, limit in zip(blocks, limits):
-                base = peak + limit
-                for half in halves:
+            pending = list(later[w + 1]) if w + 1 < count else []
+            total, mixed = None, None
+            for spot in spots:
+                base = peak + limits[spot]
+                rounded = []
+                for half in halves_of(scores[w].pop(spot)):
                     weights = jnp.exp2((half - base) * factor)
                     total = weights if total is None else total + weights
                     rounded.append(weights.astype(jnp.bfloat16))
+                if pending:
+                    ahead = pending.pop(0)
+                    scores[w + 1][ahead] = score(h, w + 1, *ahead)
+                product = jnp.dot(
+                    jnp.concatenate(rounded, axis=1), kv[spot[0], h, 1, spot[1]],
+                    preferred_element_type=jnp.float32,
+                )
+                mixed = product if mixed is None else mixed + product
+            for ahead in pending:
+                scores[w + 1][ahead] = score(h, w + 1, *ahead)
             total = jnp.sum(total, axis=1, keepdims=True)
-            mixed = jnp.dot(
-                jnp.concatenate(rounded, axis=1),
-                kv[:, h, 1, low:high].reshape(-1, D_HEAD),
-                preferred_element_type=jnp.float32,
-            )
             outs[h, w] = (mixed / total).astype(jnp.bfloat16)
             for d in peers:
                 o_copy(d, h, w).start()
-
-    for h in range(own_heads):
-        out_ref[:, columns_of(me, h)] = by_rows([outs[h, w, rows_of(me)] for w in range(count)])
-        for d in peers:
-            for w in range(count):
-                o_copy(d, h, w).wait_recv()
-            out_ref[:, columns_of(peer[d], h)] = by_rows([arrived[d - 1, h, w] for w in range(count)])
+    bring_home(own_heads - 1)
 
     for h in range(own_heads):
         for d in peers:

time: 40.5 us -> 41.4 us (1.022)
  Pallas kernels: 38.4 us -> 39.3 us
    pallas_call x1, Pallas kernels: 38.4 us -> 39.3 us  [fused(): pl.pallas_call(functools.partial(fused_kernel, times, count, own), out_sh...]
where the time goes in v5:
time: 41.4 us; the launch traced here: 41.2 us
  Pallas kernels  39.3 us (95%)
  local copies, waits for them, and re-layouts  1.87 us (5%)
    pallas_call x1, Pallas kernels, fused(): pl.pallas_call(functools.partial(fused_kernel, times, count, own), out_sh...  39.3 us
    unnamed x1, local copies, waits for them, and re-layouts  1.87 us

profile of v5, /device:TPU:0, one launch (start us, length us, event | category | flops | bytes accessed | tf_op | source)
XLA Modules:
  0.0 41.2 jit_solution(1021004286187142167)
XLA Ops:
  0.0 39.3 %shard_map.46 = bf16[256,1024]{1,0:T(8,128)(2,1)} custom-call(bf16[256,1024]{1,0:T(8,128)(2,1)} %q_hbm.1, bf16[256,1024]{1,0:T(8,128)(2,1)} %k_hbm.1, bf16[256,1024]{1,0:T(8,128)(2,1)} %v_hbm.1, s32[1,27]{1,0:T(1,128)} %bitcast.1), custom_call_target="tpu_custom_call" | custom-call | flops 8053063680 | bytes 2097152 | tf_op jit(solution)/shard_map/pallas_call | solution.py:424
  39.3 1.9 %copy.6 = bf16[256,1024]{1,0:T(8,128)(2,1)} copy(bf16[256,1024]{1,0:T(8,128)(2,1)} %shard_map.46) | data formatting | bytes 1048576

commit v6 on v3

--- a/solution.py
+++ b/solution.py
@@ -177,19 +177,19 @@
     def to(d):
         return {"spatial": peer[d]}
 
-    def kv_copy(d, h, rows):
+    def kv_copy(d, h, shard):
         return pltpu.make_async_remote_copy(
             src_ref=stage_kv.at[d - 1, h],
-            dst_ref=kv.at[1, h, :, :, rows],
+            dst_ref=kv.at[1, h, shard],
             send_sem=kv_send.at[d - 1, h],
             recv_sem=kv_recv.at[d - 1, h],
             device_id=to(d), device_id_type=MESH,
         )
 
-    def q_copy(d, h, rows):
+    def q_copy(d, h, shard):
         return pltpu.make_async_remote_copy(
             src_ref=stage_q.at[d - 1, h],
-            dst_ref=qs.at[h, :, rows],
+            dst_ref=qs.at[h, shard],
             send_sem=q_send.at[d - 1, h],
             recv_sem=q_recv.at[d - 1, h],
             device_id=to(d), device_id_type=MESH,
@@ -205,10 +205,9 @@
         )
 
     def z_copy(side, d, h):
-        rows = rows_of(peer[d])
         return pltpu.make_async_remote_copy(
-            src_ref=kv.at[1, h, :, :, rows],
-            dst_ref=kv.at[2 * side, h, :, :, rows],
+            src_ref=kv.at[1, h, peer[d]],
+            dst_ref=kv.at[2 * side, h, peer[d]],
             send_sem=z_send.at[side, d, h],
             recv_sem=z_recv.at[side, d, h],
             device_id={"temporal": t + 1 - 2 * side}, device_id_type=MESH,
@@ -261,7 +260,7 @@
                 if d:
                     stage_kv[d - 1, h, i, w] = piece
                 else:
-                    kv[1, h, i, w, rows_of(me)] = piece
+                    kv[1, h, me, i, w] = piece
 
     def lay_q(d, h):
         in_copy(2, d, h).wait()
@@ -269,7 +268,7 @@
             if d:
                 stage_q[d - 1, h, w] = piece
             else:
-                qs[h, w, rows_of(me)] = piece
+                qs[h, me, w] = piece
 
     def forward(d, h):
         for side in range(2):
@@ -295,7 +294,7 @@
     forward(0, 0)
     for d in peers:
         lay_kv(d, 0)
-        kv_copy(d, 0, rows_of(me)).start()
+        kv_copy(d, 0, me).start()
     for d in peers:
         w_copy(d, me).start()
     for h in range(1, own_heads):
@@ -309,22 +308,28 @@
 
     for h in range(own_heads):
         for d in peers:
-            kv_copy(d, h, rows_of(peer[d])).wait_recv()
+            kv_copy(d, h, peer[d]).wait_recv()
             if early(d, h):
                 forward(d, h)
             if h + 1 < own_heads:
-                kv_copy(d, h + 1, rows_of(me)).start()
+                kv_copy(d, h + 1, me).start()
             else:
-                q_copy(d, 0, rows_of(me)).start()
+                q_copy(d, 0, me).start()
     for d in peers:
         w_copy(d, peer[d]).wait_recv()
 
+    def window_of(h, i, low, high):
+        return jnp.concatenate(
+            [kv[p, h, f, i, c] for p in range(3) for c in range(low, high) for f in range(count)],
+            axis=0,
+        )
+
     factor = math.log2(math.e) / math.sqrt(D_HEAD)
     for h in range(own_heads):
         for d in peers:
-            q_copy(d, h, rows_of(peer[d])).wait_recv()
+            q_copy(d, h, peer[d]).wait_recv()
             if h + 1 < own_heads:
-                q_copy(d, h + 1, rows_of(me)).start()
+                q_copy(d, h + 1, me).start()
         for side in range(2):
             @pl.when(can_take[side])
             def _(side=side):
@@ -336,10 +341,10 @@
                     forward(d, h + 1)
         for w in range(count):
             low, high = max(w - 1, 0), min(w + 2, count)
-            query = qs[h, w]
+            query = qs[h, :, w].reshape(-1, D_HEAD)
             pattern = win[w, 0:1, :]
             wide = high - low
-            keys = kv[:, h, 0, low:high].reshape(-1, D_HEAD)
+            keys = window_of(h, 0, low, high)
             scores = lax.dot_general(
                 query, keys, (((1,), (1,)), ((), ())), preferred_element_type=jnp.float32
             )
@@ -370,7 +375,7 @@
             total = jnp.sum(total, axis=1, keepdims=True)
             mixed = jnp.dot(
                 jnp.concatenate(rounded, axis=1),
-                kv[:, h, 1, low:high].reshape(-1, D_HEAD),
+                window_of(h, 1, low, high),
                 preferred_element_type=jnp.float32,
             )
             outs[h, w] = (mixed / total).astype(jnp.bfloat16)
@@ -386,8 +391,8 @@
 
     for h in range(own_heads):
         for d in peers:
-            kv_copy(d, h, rows_of(me)).wait_send()
-            q_copy(d, h, rows_of(me)).wait_send()
+            kv_copy(d, h, me).wait_send()
+            q_copy(d, h, me).wait_send()
             for w in range(count):
                 o_copy(d, h, w).wait_send()
         for side in range(2):
@@ -419,8 +424,8 @@
             pltpu.VMEM((1, window.size), jnp.int32),
             pltpu.VMEM((count - 1, own, 2, count, part, D_HEAD), jnp.bfloat16),
             pltpu.VMEM((count - 1, own, count, part, D_HEAD), jnp.bfloat16),
-            pltpu.VMEM((3, own, 2, count, tokens, D_HEAD), jnp.bfloat16),
-            pltpu.VMEM((own, count, tokens, D_HEAD), jnp.bfloat16),
+            pltpu.VMEM((3, own, count, 2, count, part, D_HEAD), jnp.bfloat16),
+            pltpu.VMEM((own, count, count, part, D_HEAD), jnp.bfloat16),
             pltpu.VMEM((own, count, tokens, D_HEAD), jnp.bfloat16),
             pltpu.VMEM((count - 1, own, count, part, D_HEAD), jnp.bfloat16),
             pltpu.VMEM((count, 8, 128), jnp.int32),

time: 40.5 us -> 40.5 us (level)
  no operation moved by 1% of the time
where the time goes in v6:
time: 40.5 us; the launch traced here: 40.3 us
  Pallas kernels  38.4 us (95%)
  local copies, waits for them, and re-layouts  1.87 us (5%)
    pallas_call x1, Pallas kernels, fused(): pl.pallas_call(functools.partial(fused_kernel, times, count, own), out_sh...  38.4 us
    unnamed x1, local copies, waits for them, and re-layouts  1.87 us

profile of v6, /device:TPU:0, one launch (start us, length us, event | category | flops | bytes accessed | tf_op | source)
XLA Modules:
  0.0 40.3 jit_solution(2079750974732182002)
XLA Ops:
  0.0 38.4 %shard_map.46 = bf16[256,1024]{1,0:T(8,128)(2,1)} custom-call(bf16[256,1024]{1,0:T(8,128)(2,1)} %q_hbm.1, bf16[256,1024]{1,0:T(8,128)(2,1)} %k_hbm.1, bf16[256,1024]{1,0:T(8,128)(2,1)} %v_hbm.1, s32[1,27]{1,0:T(1,128)} %bitcast.1), custom_call_target="tpu_custom_call" | custom-call | flops 8053063680 | bytes 2097152 | tf_op jit(solution)/shard_map/pallas_call | solution.py:415
  38.4 1.9 %copy.6 = bf16[256,1024]{1,0:T(8,128)(2,1)} copy(bf16[256,1024]{1,0:T(8,128)(2,1)} %shard_map.46) | data formatting | bytes 1048576

commit v7 on v6

--- a/solution.py
+++ b/solution.py
@@ -168,9 +168,6 @@
     peers = range(1, count)
     peer = [flipped(me, d) for d in range(count)]
 
-    def rows_of(index):
-        return pl.ds(pl.multiple_of(index * part, part), part)
-
     def columns_of(index, h):
         return pl.ds(pl.multiple_of((index * own_heads + h) * D_HEAD, D_HEAD), D_HEAD)
 
@@ -213,32 +210,34 @@
             device_id={"temporal": t + 1 - 2 * side}, device_id_type=MESH,
         )
 
-    def o_copy(d, h, w):
+    def o_parts(h):
+        half = max(count // 2, 1)
+        return [(0, count)] if h + 1 < own_heads or half == count else [(0, half), (half, count - half)]
+
+    def o_copy(d, h, j):
+        tiles = pl.ds(*o_parts(h)[j])
         return pltpu.make_async_remote_copy(
-            src_ref=outs.at[h, w, rows_of(peer[d])],
-            dst_ref=arrived.at[d - 1, h, w],
-            send_sem=o_send.at[d - 1, h, w],
-            recv_sem=o_recv.at[d - 1, h, w],
+            src_ref=outs.at[h, peer[d], tiles],
+            dst_ref=arrived.at[d - 1, h, tiles],
+            send_sem=o_send.at[d - 1, h, j],
+            recv_sem=o_recv.at[d - 1, h, j],
             device_id=to(d), device_id_type=MESH,
         )
 
-    def in_copy(i, d, h):
-        here = columns_of(peer[d], h)
+    def in_copy(i, d):
+        wide = own_heads * D_HEAD
+        here = pl.ds(pl.multiple_of(peer[d] * wide, wide), wide)
         return pltpu.make_async_copy(
-            (k_hbm, v_hbm, q_hbm)[i].at[:, here],
-            (k_ref, v_ref, q_ref)[i].at[:, here],
-            in_sem.at[i, d, h],
-        )
-
-    for h in range(own_heads):
-        for d in range(count):
-            for i in range(2):
-                in_copy(i, d, h).start()
-    win_copy = pltpu.make_async_copy(win_hbm, win_ref, win_sem)
+            (k_hbm, v_hbm)[i].at[:, here], (k_ref, v_ref)[i].at[:, here], in_sem.at[i, d]
+        )
+
+    for d in range(count):
+        for i in range(2):
+            in_copy(i, d).start()
+    win_copy = pltpu.make_async_copy(win_hbm, win_ref, win_sem.at[0])
     win_copy.start()
-    for h in range(own_heads):
-        for d in range(count):
-            in_copy(2, d, h).start()
+    q_in = pltpu.make_async_copy(q_hbm, q_ref, win_sem.at[1])
+    q_in.start()
 
     can_send = (t < times - 1, t > 0)
     can_take = (t > 0, t < times - 1)
@@ -255,7 +254,8 @@
 
     def lay_kv(d, h):
         for i, ref in enumerate((k_ref, v_ref)):
-            in_copy(i, d, h).wait()
+            if h == 0:
+                in_copy(i, d).wait()
             for w, piece in enumerate(by_tiles(ref[:, columns_of(peer[d], h)], count)):
                 if d:
                     stage_kv[d - 1, h, i, w] = piece
@@ -263,7 +263,8 @@
                     kv[1, h, me, i, w] = piece
 
     def lay_q(d, h):
-        in_copy(2, d, h).wait()
+        if d == 0 and h == 0:
+            q_in.wait()
         for w, piece in enumerate(by_tiles(q_ref[:, columns_of(peer[d], h)], count)):
             if d:
                 stage_q[d - 1, h, w] = piece
@@ -318,6 +319,13 @@
     for d in peers:
         w_copy(d, peer[d]).wait_recv()
 
+    def bring_home(h):
+        out_ref[:, columns_of(me, h)] = by_rows([outs[h, me, w] for w in range(count)])
+        for d in peers:
+            for j in range(len(o_parts(h))):
+                o_copy(d, h, j).wait_recv()
+            out_ref[:, columns_of(peer[d], h)] = by_rows([arrived[d - 1, h, w] for w in range(count)])
+
     def window_of(h, i, low, high):
         return jnp.concatenate(
             [kv[p, h, f, i, c] for p in range(3) for c in range(low, high) for f in range(count)],
@@ -330,6 +338,8 @@
             q_copy(d, h, peer[d]).wait_recv()
             if h + 1 < own_heads:
                 q_copy(d, h + 1, me).start()
+        if h:
+            bring_home(h - 1)
         for side in range(2):
             @pl.when(can_take[side])
             def _(side=side):
@@ -378,23 +388,22 @@
                 window_of(h, 1, low, high),
                 preferred_element_type=jnp.float32,
             )
-            outs[h, w] = (mixed / total).astype(jnp.bfloat16)
-            for d in peers:
-                o_copy(d, h, w).start()
-
-    for h in range(own_heads):
-        out_ref[:, columns_of(me, h)] = by_rows([outs[h, w, rows_of(me)] for w in range(count)])
-        for d in peers:
-            for w in range(count):
-                o_copy(d, h, w).wait_recv()
-            out_ref[:, columns_of(peer[d], h)] = by_rows([arrived[d - 1, h, w] for w in range(count)])
+            attended = (mixed / total).astype(jnp.bfloat16)
+            for f in range(count):
+                outs[h, f, w] = attended[f * part : (f + 1) * part]
+            for j, (first, number) in enumerate(o_parts(h)):
+                if w == first + number - 1:
+                    for d in peers:
+                        o_copy(d, h, j).start()
+
+    bring_home(own_heads - 1)
 
     for h in range(own_heads):
         for d in peers:
             kv_copy(d, h, me).wait_send()
             q_copy(d, h, me).wait_send()
-            for w in range(count):
-                o_copy(d, h, w).wait_send()
+            for j in range(len(o_parts(h))):
+                o_copy(d, h, j).wait_send()
         for side in range(2):
             @pl.when(can_send[side])
             def _(side=side):
@@ -426,15 +435,15 @@
             pltpu.VMEM((count - 1, own, count, part, D_HEAD), jnp.bfloat16),
             pltpu.VMEM((3, own, count, 2, count, part, D_HEAD), jnp.bfloat16),
             pltpu.VMEM((own, count, count, part, D_HEAD), jnp.bfloat16),
-            pltpu.VMEM((own, count, tokens, D_HEAD), jnp.bfloat16),
+            pltpu.VMEM((own, count, count, part, D_HEAD), jnp.bfloat16),
             pltpu.VMEM((count - 1, own, count, part, D_HEAD), jnp.bfloat16),
             pltpu.VMEM((count, 8, 128), jnp.int32),
             dma((count - 1, own)), dma((count - 1, own)),
             dma((count - 1, own)), dma((count - 1, own)),
             dma((2, count, own)), dma((2, count, own)),
-            dma((count - 1, own, count)), dma((count - 1, own, count)),
+            dma((count - 1, own, 2)), dma((count - 1, own, 2)),
             dma((count - 1,)), dma((count - 1,)),
-            dma((3, count, own)), dma,
+            dma((2, count)), dma((2,)),
         ],
         compiler_params=pltpu.CompilerParams(
             collective_id=0, has_side_effects=True, vmem_limit_bytes=60 * 2**20

time: 40.5 us -> 41 us (1.012)
  Pallas kernels: 38.4 us -> 39 us
    pallas_call x1, Pallas kernels: 38.4 us -> 39 us  [fused(): pl.pallas_call(functools.partial(fused_kernel, times, count, own), out_sh...]
where the time goes in v7:
time: 41 us; the launch traced here: 40.9 us
  Pallas kernels  39 us (95%)
  local copies, waits for them, and re-layouts  1.87 us (5%)
    pallas_call x1, Pallas kernels, fused(): pl.pallas_call(functools.partial(fused_kernel, times, count, own), out_sh...  39 us
    unnamed x1, local copies, waits for them, and re-layouts  1.87 us

profile of v7, /device:TPU:0, one launch (start us, length us, event | category | flops | bytes accessed | tf_op | source)
XLA Modules:
  0.0 40.9 jit_solution(12154044473950864688)
XLA Ops:
  0.0 39.0 %shard_map.46 = bf16[256,1024]{1,0:T(8,128)(2,1)} custom-call(bf16[256,1024]{1,0:T(8,128)(2,1)} %q_hbm.1, bf16[256,1024]{1,0:T(8,128)(2,1)} %k_hbm.1, bf16[256,1024]{1,0:T(8,128)(2,1)} %v_hbm.1, s32[1,27]{1,0:T(1,128)} %bitcast.1), custom_call_target="tpu_custom_call" | custom-call | flops 8053063680 | bytes 2097152 | tf_op jit(solution)/shard_map/pallas_call | solution.py:424
  39.0 1.9 %copy.6 = bf16[256,1024]{1,0:T(8,128)(2,1)} copy(bf16[256,1024]{1,0:T(8,128)(2,1)} %shard_map.46) | data formatting | bytes 1048576

commit v8 on v6

--- a/solution.py
+++ b/solution.py
@@ -155,6 +155,11 @@
     ).astype(jnp.bfloat16)
 
 
+def column_groups(count):
+    first = min(2, count)
+    return [(0, first)] + [(c, 1) for c in range(first, count)]
+
+
 def fused_kernel(
     times, count, own_heads,
     q_hbm, k_hbm, v_hbm, win_hbm, out_ref,
@@ -204,12 +209,16 @@
             device_id=to(d), device_id_type=MESH,
         )
 
-    def z_copy(side, d, h):
+    def groups(h):
+        return column_groups(count) if h + 1 == own_heads else [(0, count)]
+
+    def z_copy(side, d, h, j):
+        tiles = pl.ds(*groups(h)[j])
         return pltpu.make_async_remote_copy(
-            src_ref=kv.at[1, h, peer[d]],
-            dst_ref=kv.at[2 * side, h, peer[d]],
-            send_sem=z_send.at[side, d, h],
-            recv_sem=z_recv.at[side, d, h],
+            src_ref=kv.at[1, h, peer[d], :, tiles],
+            dst_ref=kv.at[2 * side, h, peer[d], :, tiles],
+            send_sem=z_send.at[side, d, h, j],
+            recv_sem=z_recv.at[side, d, h, j],
             device_id={"temporal": t + 1 - 2 * side}, device_id_type=MESH,
         )
 
@@ -270,11 +279,25 @@
             else:
                 qs[h, me, w] = piece
 
-    def forward(d, h):
+    def forward(d, h, some=slice(None)):
         for side in range(2):
             @pl.when(can_send[side])
             def _(side=side):
-                z_copy(side, d, h).start()
+                for j in range(len(groups(h)))[some]:
+                    z_copy(side, d, h, j).start()
+
+    def forward_late(h, some):
+        for d in range(count):
+            if h < own_heads and not early(d, h):
+                forward(d, h, some)
+
+    def take(h, some=slice(None)):
+        for side in range(2):
+            @pl.when(can_take[side])
+            def _(side=side):
+                for j in range(len(groups(h)))[some]:
+                    for d in range(count):
+                        z_copy(side, d, h, j).wait_recv()
 
     lay_kv(0, 0)
     win_copy.wait()
@@ -318,6 +341,13 @@
     for d in peers:
         w_copy(d, peer[d]).wait_recv()
 
+    def bring_home(h):
+        out_ref[:, columns_of(me, h)] = by_rows([outs[h, w, rows_of(me)] for w in range(count)])
+        for d in peers:
+            for w in range(count):
+                o_copy(d, h, w).wait_recv()
+            out_ref[:, columns_of(peer[d], h)] = by_rows([arrived[d - 1, h, w] for w in range(count)])
+
     def window_of(h, i, low, high):
         return jnp.concatenate(
             [kv[p, h, f, i, c] for p in range(3) for c in range(low, high) for f in range(count)],
@@ -330,16 +360,17 @@
             q_copy(d, h, peer[d]).wait_recv()
             if h + 1 < own_heads:
                 q_copy(d, h + 1, me).start()
-        for side in range(2):
-            @pl.when(can_take[side])
-            def _(side=side):
-                for d in range(count):
-                    z_copy(side, d, h).wait_recv()
-        if h + 1 < own_heads:
-            for d in range(count):
-                if not early(d, h + 1):
-                    forward(d, h + 1)
+        last = h + 1 == own_heads
+        if not last:
+            take(h)
+            forward_late(h + 1, slice(0, 2))
         for w in range(count):
+            if last and w < len(groups(h)):
+                if w + 1 == len(groups(h)) and h:
+                    bring_home(h - 1)
+                take(h, slice(w, w + 1))
+            if not last and w == count // 2:
+                forward_late(h + 1, slice(2, None))
             low, high = max(w - 1, 0), min(w + 2, count)
             query = qs[h, :, w].reshape(-1, D_HEAD)
             pattern = win[w, 0:1, :]
@@ -382,12 +413,7 @@
             for d in peers:
                 o_copy(d, h, w).start()
 
-    for h in range(own_heads):
-        out_ref[:, columns_of(me, h)] = by_rows([outs[h, w, rows_of(me)] for w in range(count)])
-        for d in peers:
-            for w in range(count):
-                o_copy(d, h, w).wait_recv()
-            out_ref[:, columns_of(peer[d], h)] = by_rows([arrived[d - 1, h, w] for w in range(count)])
+    bring_home(own_heads - 1)
 
     for h in range(own_heads):
         for d in peers:
@@ -399,7 +425,8 @@
             @pl.when(can_send[side])
             def _(side=side):
                 for d in range(count):
-                    z_copy(side, d, h).wait_send()
+                    for j in range(len(groups(h))):
+                        z_copy(side, d, h, j).wait_send()
     for d in peers:
         w_copy(d, me).wait_send()
 
@@ -409,6 +436,7 @@
     tokens, channels = queries.shape
     own = channels // (D_HEAD * count)
     part = tokens // count
+    groups = len(column_groups(count))
     vmem = pl.BlockSpec(memory_space=pltpu.VMEM)
     dma = pltpu.SemaphoreType.DMA
     pairs = own * count * (3 * count - 2) * 3 * tokens * tokens * D_HEAD
@@ -431,7 +459,7 @@
             pltpu.VMEM((count, 8, 128), jnp.int32),
             dma((count - 1, own)), dma((count - 1, own)),
             dma((count - 1, own)), dma((count - 1, own)),
-            dma((2, count, own)), dma((2, count, own)),
+            dma((2, count, own, groups)), dma((2, count, own, groups)),
             dma((count - 1, own, count)), dma((count - 1, own, count)),
             dma((count - 1,)), dma((count - 1,)),
             dma((3, count, own)), dma,

time: 40.5 us -> 40.1 us (level)
  no operation moved by 1% of the time
where the time goes in v8:
time: 40.1 us; the launch traced here: 39.9 us
  Pallas kernels  38 us (95%)
  local copies, waits for them, and re-layouts  1.87 us (5%)
    pallas_call x1, Pallas kernels, fused(): pl.pallas_call(functools.partial(fused_kernel, times, count, own), out_sh...  38 us
    unnamed x1, local copies, waits for them, and re-layouts  1.87 us

profile of v8, /device:TPU:0, one launch (start us, length us, event | category | flops | bytes accessed | tf_op | source)
XLA Modules:
  0.0 39.9 jit_solution(13994494723588744758)
XLA Ops:
  0.0 38.0 %shard_map.46 = bf16[256,1024]{1,0:T(8,128)(2,1)} custom-call(bf16[256,1024]{1,0:T(8,128)(2,1)} %q_hbm.1, bf16[256,1024]{1,0:T(8,128)(2,1)} %k_hbm.1, bf16[256,1024]{1,0:T(8,128)(2,1)} %v_hbm.1, s32[1,27]{1,0:T(1,128)} %bitcast.1), custom_call_target="tpu_custom_call" | custom-call | flops 8053063680 | bytes 2097152 | tf_op jit(solution)/shard_map/pallas_call | solution.py:443
  38.0 1.9 %copy.6 = bf16[256,1024]{1,0:T(8,128)(2,1)} copy(bf16[256,1024]{1,0:T(8,128)(2,1)} %shard_map.46) | data formatting | bytes 1048576

commit v9 on v8

--- a/solution.py
+++ b/solution.py
@@ -431,6 +431,32 @@
         w_copy(d, me).wait_send()
 
 
+def settle_kernel(source, result, sems):
+    parts = sems.shape[0]
+    rows = source.shape[0] // parts
+    copies = [
+        pltpu.make_async_copy(
+            source.at[pl.ds(i * rows, rows)], result.at[pl.ds(i * rows, rows)], sems.at[i]
+        )
+        for i in range(parts)
+    ]
+    for copy in copies:
+        copy.start()
+    for copy in copies:
+        copy.wait()
+
+
+def settle(array):
+    return pl.pallas_call(
+        settle_kernel,
+        out_shape=jax.ShapeDtypeStruct(array.shape, array.dtype),
+        in_specs=[pl.BlockSpec(memory_space=pl.ANY)],
+        out_specs=pl.BlockSpec(memory_space=pl.ANY),
+        scratch_shapes=[pltpu.SemaphoreType.DMA((8,))],
+        compiler_params=pltpu.CompilerParams(vmem_limit_bytes=60 * 2**20),
+    )(array)
+
+
 def fused(queries, keys, values, window):
     count, times = lax.axis_size("spatial"), lax.axis_size("temporal")
     tokens, channels = queries.shape
@@ -479,7 +505,7 @@
     heads_here = channels // D_HEAD
     whole_tiles = window.shape[1] == 1 and window.shape[2] == 1 and tokens == TILE_T * TILE_H * TILE_W
     if whole_tiles and count & (count - 1) == 0 and heads_here % count == 0:
-        return fused(queries, keys, values, window)
+        return settle(fused(queries, keys, values, window))
     return gathered(queries, keys, values, window)
 
 

time: 40.1 us -> 55.3 us (1.38)
  Pallas kernels: 38 us -> 55.1 us
  local copies, waits for them, and re-layouts: 1.87 us -> 0 us
    pallas_call x0 -> x1, Pallas kernels: none -> 17.1 us  [settle(): pl.pallas_call(settle_kernel, out_shape=jax.ShapeDtypeStruct(array.shape,...]
    unnamed x1 -> x0, local copies, waits for them, and re-layouts: 1.87 us -> none
where the time goes in v9:
time: 55.3 us; the launch traced here: 55.1 us
  Pallas kernels  55.1 us (100%)
    pallas_call x1, Pallas kernels, fused(): pl.pallas_call(functools.partial(fused_kernel, times, count, own), out_sh...  38 us
    pallas_call x1, Pallas kernels, settle(): pl.pallas_call(settle_kernel, out_shape=jax.ShapeDtypeStruct(array.shape,...  17.1 us

profile of v9, /device:TPU:0, one launch (start us, length us, event | category | flops | bytes accessed | tf_op | source)
XLA Modules:
  0.0 55.1 jit_solution(10865347206196859040)
XLA Ops:
  0.0 38.0 %shard_map.46.source = bf16[256,1024]{1,0:T(8,128)(2,1)} custom-call(bf16[256,1024]{1,0:T(8,128)(2,1)} %q_hbm.1, bf16[256,1024]{1,0:T(8,128)(2,1)} %k_hbm.1, bf16[256,1024]{1,0:T(8,128)(2,1)} %v_hbm.1, s32[1,27]{1,0:T(1,128)} %bitcast.1), custom_call_target="tpu_custom_call" | custom-call | flops 8053063680 | bytes 2097152 | tf_op jit(solution)/shard_map/pallas_call | solution.py:469
  38.0 17.1 %shard_map.47 = bf16[256,1024]{1,0:T(8,128)(2,1)} custom-call(bf16[256,1024]{1,0:T(8,128)(2,1)} %shard_map.46.source), custom_call_target="tpu_custom_call" | custom-call | tf_op jit(solution)/shard_map/pallas_call | solution.py:450
